TPU v7x, 32 devices: a whole 2x2x4 slice. The times are simulated.
32 devices in a mesh: dp: 2 (over core), fsdp: 16 (over z, y, x).
Axes of the slice: x: 2, y: 2, z: 4, core: 2. Of those that a mesh axis runs over, the one named last changes fastest.
Arguments:
- patches: bfloat16 [128, 576, 768], P(('dp', 'fsdp')), may hold values from -6 to 6
- resolution: int32 [128], P(('dp', 'fsdp')), may hold values 0 or 1
- labels: int32 [128], P(('dp', 'fsdp')), may hold values from 0 to 999
- dense_weights: float32 [384, 3840], P(None, ('dp', 'fsdp')), may hold values from -0.20412415 to 0.20412415
- attention: float32 [3, 384, 1536], P(None, None, ('dp', 'fsdp')), may hold values from -1.1547005 to 1.1547005
- router: float32 [2, 384, 128], P(None, 'dp', 'fsdp'), may hold values from -0.21875 to 0.21875
- expert_in: float32 [2, 128, 384, 1536], P(None, 'fsdp', None, 'dp'), may hold values from -4 to 4
- expert_out: float32 [2, 128, 1536, 384], P(None, 'fsdp', 'dp'), may hold values from -0.21875 to 0.21875
- classifier: float32 [385, 1000], replicated, may hold values from -0.3125 to 0.3125
- norm_table: float32 [210, 384], replicated, may hold values from -2 to 2
- dense_weights_first: float32 [384, 3840], P(None, ('dp', 'fsdp')), may hold values from -3.7252903e-08 to 3.7252903e-08
- dense_weights_second: float32 [384, 3840], P(None, ('dp', 'fsdp')), may hold values from 1.7200905e-16 to 6.8672815e-16
- attention_first: float32 [3, 384, 1536], P(None, None, ('dp', 'fsdp')), may hold values from -2.3841858e-07 to 2.3841858e-07
- attention_second: float32 [3, 384, 1536], P(None, None, ('dp', 'fsdp')), may hold values from 8.600452e-15 to 3.433641e-14
- router_first: float32 [2, 384, 128], P(None, 'dp', 'fsdp'), may hold values from -3.7252903e-08 to 3.7252903e-08
- router_second: float32 [2, 384, 128], P(None, 'dp', 'fsdp'), may hold values from 1.7200905e-16 to 6.8672815e-16
- expert_in_first: float32 [2, 128, 384, 1536], P(None, 'fsdp', None, 'dp'), may hold values from -1.6298145e-09 to 1.6298145e-09
- expert_in_second: float32 [2, 128, 384, 1536], P(None, 'fsdp', None, 'dp'), may hold values from 1.1870587e-18 to 4.741694e-18
- expert_out_first: float32 [2, 128, 1536, 384], P(None, 'fsdp', 'dp'), may hold values from -3.7252903e-08 to 3.7252903e-08
- expert_out_second: float32 [2, 128, 1536, 384], P(None, 'fsdp', 'dp'), may hold values from 1.7200905e-16 to 6.8672815e-16
- classifier_first: float32 [385, 1000], replicated, may hold values from -3.7252903e-08 to 3.7252903e-08
- classifier_second: float32 [385, 1000], replicated, may hold values from 1.7200905e-16 to 6.8672815e-16
- norm_table_first: float32 [210, 384], replicated, may hold values from -3.7252903e-08 to 3.7252903e-08
- norm_table_second: float32 [210, 384], replicated, may hold values from 1.7200905e-16 to 6.8672815e-16
Outputs:
- loss: float32 [], replicated
- grad_norm: float32 [], replicated
- new_dense_weights: float32 [384, 3840], P(None, ('dp', 'fsdp'))
- new_dense_weights_first: float32 [384, 3840], P(None, ('dp', 'fsdp'))
- new_dense_weights_second: float32 [384, 3840], P(None, ('dp', 'fsdp'))
- new_attention: float32 [3, 384, 1536], P(None, None, ('dp', 'fsdp'))
- new_attention_first: float32 [3, 384, 1536], P(None, None, ('dp', 'fsdp'))
- new_attention_second: float32 [3, 384, 1536], P(None, None, ('dp', 'fsdp'))
- new_router: float32 [2, 384, 128], P(None, 'dp', 'fsdp')
- new_router_first: float32 [2, 384, 128], P(None, 'dp', 'fsdp')
- new_router_second: float32 [2, 384, 128], P(None, 'dp', 'fsdp')
- new_expert_in: float32 [2, 128, 384, 1536], P(None, 'fsdp', None, 'dp')
- new_expert_in_first: float32 [2, 128, 384, 1536], P(None, 'fsdp', None, 'dp')
- new_expert_in_second: float32 [2, 128, 384, 1536], P(None, 'fsdp', None, 'dp')
- new_expert_out: float32 [2, 128, 1536, 384], P(None, 'fsdp', 'dp')
- new_expert_out_first: float32 [2, 128, 1536, 384], P(None, 'fsdp', 'dp')
- new_expert_out_second: float32 [2, 128, 1536, 384], P(None, 'fsdp', 'dp')
- new_classifier: float32 [385, 1000], replicated
- new_classifier_first: float32 [385, 1000], replicated
- new_classifier_second: float32 [385, 1000], replicated
- new_norm_table: float32 [210, 384], replicated
- new_norm_table_first: float32 [210, 384], replicated
- new_norm_table_second: float32 [210, 384], replicated
All inputs are finite; a program needn't handle non-finite values. No bound on the sum of `resolution` on one device may be relied on, other than what follows from the above.
Results may differ from a plain program's by a relative error of at most 0.022.
Values may be sent and summed in bfloat16 or wider, within the bound.
A program may use at most 512 MiB of HBM per device.

v0:
```python
import functools

import jax
import jax.numpy as jnp
from jax import lax
from jax.experimental import pallas as pl
from jax.experimental.pallas import tpu as pltpu
from jax.sharding import PartitionSpec as P

HEADS = 6
FF = 1536
G_LO = 14
G_HI = 24
LEN = 576
LEN_LO = 196
ROWS_LO = 208
STEP = 10


LN_EPS = 1e-06
CLIP_NORM = 0.001
LEARN_RATE = 0.05
ATTENTION_RATE = 0.15
EXPERT_RATE = 1.0
TABLE_RATE = 0.5
BETA_ONE = 0.9
BETA_TWO = 0.95
ADAM_EPS = 1e-10
WEIGHT_DECAY = 0.1
SMOOTH = 0.1
NEG_FILL = -1e30
PRECISE = lax.Precision.HIGHEST
F32 = jnp.float32
BF16 = jnp.bfloat16
VMEM_BYTES = 60 * 1024 * 1024


def interp_matrix():
    rows = jnp.arange(G_HI, dtype=jnp.float32)[:, None]
    cols = jnp.arange(G_LO, dtype=jnp.float32)[None, :]
    weight = jnp.maximum(0.0, 1.0 - jnp.abs(rows * (G_LO - 1) - cols * (G_HI - 1)) / (G_HI - 1))
    return (weight[:, None, :, None] * weight[None, :, None, :]).reshape(G_HI * G_HI, G_LO * G_LO)


def matmul(left, right, form):
    return jnp.einsum(form, left, right, preferred_element_type=jnp.float32)


def contract(left, right, left_dim, right_dim):
    return lax.dot_general(
        left, right, (((left_dim,), (right_dim,)), ((), ())), preferred_element_type=F32
    )


def nn(left, right):
    return contract(left, right, 1, 0)


def nt(left, right):
    return contract(left, right, 1, 1)


def tn(left, right):
    return contract(left, right, 0, 0)


def normalise(values):
    center = values - jnp.mean(values, -1, keepdims=True)
    rate = lax.rsqrt(jnp.mean(center * center, -1, keepdims=True) + LN_EPS)
    return center * rate, rate


def normalise_back(unit, rate, gain, grad):
    scaled = grad * gain
    inner = scaled - jnp.mean(scaled, -1, keepdims=True)
    grad_in = rate * (inner - unit * jnp.mean(scaled * unit, -1, keepdims=True))
    return (
        grad_in,
        jnp.sum(grad * unit, 0, keepdims=True),
        jnp.sum(grad, 0, keepdims=True),
    )


def row_number(shape):
    return lax.broadcasted_iota(jnp.int32, shape, 0)


def side_masks():
    lane = lax.broadcasted_iota(jnp.int32, (1, 128), 1)
    first = (lane < 64).astype(F32)
    return (first.astype(BF16), (1.0 - first).astype(BF16))


def lanes(offset):
    return pl.ds(pl.multiple_of(offset, 128), 128)


GELU_RATE = 0.7978845608028654


def gelu(v):
    return 0.5 * v * (1.0 + jnp.tanh(GELU_RATE * (v + 0.044715 * (v * v * v))))


def gelu_both(v):
    square = v * v
    bend = jnp.tanh(GELU_RATE * (v + 0.044715 * (square * v)))
    half = 0.5 * (1.0 + bend)
    slope = half + 0.5 * v * (1.0 - bend * bend) * (GELU_RATE * (1.0 + 3 * 0.044715 * square))
    return v * half, slope


def attention_rows(rows, limit, qkv, context):
    width = context.shape[1]
    first = lax.broadcasted_iota(jnp.int32, (rows, 128), 1) < 64
    masks = side_masks()
    ones = jnp.ones((rows, 128), BF16)
    for offset in range(0, width, 128):
        query = qkv[:rows, offset : offset + 128] * BF16(0.125)
        keys = qkv[:rows, width + offset : width + offset + 128]
        values = qkv[:rows, 2 * width + offset : 2 * width + offset + 128]
        summing = jnp.concatenate([values, ones], 1)
        found = []
        for side in (0, 1):
            scores = nt(query * masks[side], keys)
            if limit is not None:
                lane = lax.broadcasted_iota(jnp.int32, (rows, rows), 1)
                scores = jnp.where(lane < limit, scores, NEG_FILL)
            raised = jnp.exp(scores - jnp.max(scores, 1, keepdims=True))
            both = nn(raised.astype(BF16), summing)
            found.append(both[:, :128] * (1.0 / both[:, 128:]))
        context[:rows, offset : offset + 128] = jnp.where(first, found[0], found[1]).astype(BF16)


def scores_back(limit, keys, values, query, grad):
    scores = nt(keys, query)
    if limit is not None:
        scores = jnp.where(row_number(scores.shape) < limit, scores, NEG_FILL)
    raised = jnp.exp(scores - jnp.max(scores, 0, keepdims=True))
    probs = raised * (1.0 / jnp.sum(raised, 0, keepdims=True))
    grad_values = nn(probs.astype(BF16), grad)
    grad_probs = nt(values, grad)
    mixed = jnp.sum(probs * grad_probs, 0, keepdims=True)
    grad_scores = (probs * (grad_probs - mixed)).astype(BF16)
    return grad_scores, nn(grad_scores, query), grad_values


def attention_rows_back(rows, limit, qkv, grad_context, grad_qkv):
    width = grad_context.shape[1]
    masks = side_masks()
    first = lax.broadcasted_iota(jnp.int32, (rows, 128), 1) < 64

    def pair(offset):
        query = qkv[:rows, lanes(offset)] * BF16(0.125)
        keys = qkv[:rows, lanes(width + offset)]
        values = qkv[:rows, lanes(2 * width + offset)]
        grad = grad_context[:rows, lanes(offset)]
        queries = [query * mask for mask in masks]
        grads = [grad * mask for mask in masks]
        if limit is None:
            grad_scores, grad_keys, grad_values = scores_back(
                limit, keys, values, jnp.concatenate(queries, 0), jnp.concatenate(grads, 0)
            )
            both = tn(grad_scores, keys)
            grad_query = jnp.where(first, both[:rows], both[rows:])
        else:
            one, two = [
                scores_back(limit, keys, values, queries[side], grads[side]) for side in (0, 1)
            ]
            grad_query = tn(one[0], keys * masks[0]) + tn(two[0], keys * masks[1])
            grad_keys, grad_values = one[1] + two[1], one[2] + two[2]
        grad_qkv[:rows, lanes(offset)] = (grad_query * 0.125).astype(BF16)
        grad_qkv[:rows, lanes(width + offset)] = grad_keys.astype(BF16)
        grad_qkv[:rows, lanes(2 * width + offset)] = grad_values.astype(BF16)

    if limit is None:

        def step(index, carry):
            pair(index * 128)
            return carry

        lax.fori_loop(0, width // 128, step, 0)
    else:
        for offset in range(0, width, 128):
            pair(offset)


def attention_forward(rows, limit, hidden, gains, weights, qkv, context):
    width = hidden.shape[1]
    unit, _ = normalise(hidden)
    normed = (unit * gains[0:1] + gains[1:2]).astype(BF16)
    qkv[:rows] = nt(normed, weights[: 3 * width]).astype(BF16)
    attention_rows(rows, limit, qkv, context)
    return hidden + nn(context[:rows], weights[3 * width :])


def attention_backward(
    rows, limit, hidden, grad_middle, gains, weights, qkv, context, hold_context, hold_qkv,
    grad_weights, grad_gains,
):
    width = hidden.shape[1]
    grad_b = grad_middle.astype(BF16)
    hold_context[:rows] = nt(grad_b, weights[3 * width :]).astype(BF16)
    grad_weights[3 * width :] += tn(context[:rows], grad_b)
    attention_rows_back(rows, limit, qkv, hold_context, hold_qkv)
    unit, rate = normalise(hidden)
    normed = (unit * gains[0:1] + gains[1:2]).astype(BF16)
    grad_weights[: 3 * width] += tn(hold_qkv[:rows], normed)
    grad_normed = nn(hold_qkv[:rows], weights[: 3 * width])
    grad_in, grad_gain, grad_bias = normalise_back(unit, rate, gains[0:1], grad_normed)
    grad_gains[0:1] += grad_gain
    grad_gains[1:2] += grad_bias
    return grad_middle + grad_in


def mlp_forward(rows, middle, gains, weights, pixels):
    unit, _ = normalise(middle)
    normed = (unit * gains[2:3] + gains[3:4]).astype(BF16)
    chunk = middle.shape[1]
    total = middle
    for start in range(0, FF, chunk):
        pre = nt(normed, weights[pixels + start : pixels + start + chunk])
        out = weights[pixels + FF + start : pixels + FF + start + chunk]
        total = total + nn(gelu(pre).astype(BF16), out)
    return total


def mlp_backward(rows, middle, grad, gains, weights, pixels, grad_weights, grad_gains):
    unit, rate = normalise(middle)
    normed = (unit * gains[2:3] + gains[3:4]).astype(BF16)
    grad_b = grad.astype(BF16)
    chunk = middle.shape[1]
    grad_normed = None
    for start in range(0, FF, chunk):
        first = slice(pixels + start, pixels + start + chunk)
        second = slice(pixels + FF + start, pixels + FF + start + chunk)
        hid, slope = gelu_both(nt(normed, weights[first]))
        grad_weights[second] += tn(hid.astype(BF16), grad_b)
        grad_pre = (nt(grad_b, weights[second]) * slope).astype(BF16)
        grad_weights[first] += tn(grad_pre, normed)
        part = nn(grad_pre, weights[first])
        grad_normed = part if grad_normed is None else grad_normed + part
    grad_in, grad_gain, grad_bias = normalise_back(unit, rate, gains[2:3], grad_normed)
    grad_gains[2:3] += grad_gain
    grad_gains[3:4] += grad_bias
    return grad + grad_in


def route(limit, middle, gains, router):
    unit, rate = normalise(middle)
    normed = (unit * gains[2:3] + gains[3:4]).astype(BF16)
    logits = nt(normed, router[...])
    masked = logits
    if limit is not None:
        masked = jnp.where(row_number(logits.shape) < limit, logits, NEG_FILL)
    raised = jnp.exp(masked - jnp.max(masked, 0, keepdims=True))
    dispatch = raised * (1.0 / jnp.sum(raised, 0, keepdims=True))
    raised = jnp.exp(logits - jnp.max(logits, 1, keepdims=True))
    combine = raised * (1.0 / jnp.sum(raised, 1, keepdims=True))
    return unit, rate, normed, dispatch, combine


def masked_rows(limit, values):
    if limit is None:
        return values
    return jnp.where(row_number(values.shape) < limit, values, 0.0)


def work_of(giga):
    return pl.CostEstimate(flops=giga * 10**9, bytes_accessed=1 << 20, transcendentals=0)


def by_image(name, body, scalars, per_image, whole, out_image, out_sum, scratch=(), pack=None):
    images = scalars[0].shape[0]
    inner = pack[0] if pack else 0
    packed = 1 if pack else 0
    counts = (
        len(scalars), len(per_image), len(whole), len(out_image), packed, len(out_sum) - inner,
        inner, len(scratch),
    )

    def kernel(*refs):
        groups, at = [], 0
        for count in counts:
            groups.append(refs[at : at + count])
            at += count
        index = pl.program_id(0)
        sums = tuple(groups[6]) + tuple(groups[5])

        @pl.when(index == 0)
        def _():
            for ref in sums:
                ref[...] = jnp.zeros_like(ref)

        numbers = [ref[index] for ref in groups[0]]
        given = (*groups[1:4], sums, groups[7])

        @pl.when(numbers[0] == 1)
        def _():
            body(LEN, None, numbers, *given)

        @pl.when(numbers[0] != 1)
        def _():
            body(ROWS_LO, LEN_LO + numbers[0], numbers, *given)

        if pack:

            @pl.when(index == images - 1)
            def _():
                def write(device, carry):
                    groups[4][0][device] = pack[3](sums, device).astype(BF16)
                    return carry

                lax.fori_loop(0, pack[1], write, 0)

    width = out_sum[0][1] if pack else 0
    pack_shapes = [(pack[1], pack[2], width)] if pack else []

    def image_spec(shape):
        return pl.BlockSpec((None,) + tuple(shape[1:]), lambda i, *_: (i, 0, 0))

    return pl.pallas_call(
        kernel,
        grid_spec=pltpu.PrefetchScalarGridSpec(
            num_scalar_prefetch=len(scalars),
            grid=(images,),
            in_specs=[image_spec(a.shape) for a in per_image]
            + [pl.BlockSpec(memory_space=pltpu.VMEM) for _ in whole],
            out_specs=[image_spec((images,) + shape) for shape, _ in out_image]
            + [pl.BlockSpec(shape, lambda i, *_: (0, 0, 0)) for shape in pack_shapes]
            + [pl.BlockSpec(shape, lambda i, *_: (0, 0)) for shape in out_sum[inner:]],
            scratch_shapes=[pltpu.VMEM(shape, F32) for shape in out_sum[:inner]] + list(scratch),
        ),
        out_shape=[jax.ShapeDtypeStruct((images,) + shape, dtype) for shape, dtype in out_image]
        + [jax.ShapeDtypeStruct(shape, BF16) for shape in pack_shapes]
        + [jax.ShapeDtypeStruct(shape, F32) for shape in out_sum[inner:]],
        compiler_params=pltpu.CompilerParams(vmem_limit_bytes=VMEM_BYTES),
        cost_estimate=work_of(images * 8),
        name=name,
    )(*scalars, *per_image, *whole)


def rows_of(ref, device, count):
    return ref[pl.ds(pl.multiple_of(device * count, 8), count)]


def padded_rows(blocks):
    rows = sum(block.shape[0] for block in blocks)
    if rows % 16:
        blocks = blocks + [jnp.zeros((-rows % 16, blocks[0].shape[1]), F32)]
    return jnp.concatenate(blocks, 0) if len(blocks) > 1 else blocks[0]


def up_16(count):
    return count + -count % 16


def first_forward(resolution, patches, dense, attention, positions, gains, width):
    pixels = patches.shape[2]

    def body(rows, limit, numbers, images, whole, outs, sums, scratch):
        dense_ref, attention_ref, position_ref, gain_ref = whole
        start, qkv, context, middle, last = outs
        place = position_ref[0 if limit is not None else 1, :rows]
        embedded = masked_rows(limit, nn(images[0][:rows], dense_ref[:pixels]) + place)
        start[:rows] = embedded
        middle_rows = attention_forward(
            rows, limit, embedded, gain_ref, attention_ref, qkv, context
        )
        middle[:rows] = middle_rows
        last[:rows] = mlp_forward(rows, middle_rows, gain_ref, dense_ref, pixels)

    return by_image(
        "first_forward",
        body,
        [resolution],
        [patches],
        [dense, attention, positions, gains],
        [
            ((LEN, width), F32),
            ((LEN, 3 * width), BF16),
            ((LEN, width), BF16),
            ((LEN, width), F32),
            ((LEN, width), F32),
        ],
        [],
    )


def sparse_forward(resolution, hidden, mixing, attention, router, gains):
    width = hidden.shape[2]
    experts = router.shape[0]

    def body(rows, limit, numbers, images, whole, outs, sums, scratch):
        attention_ref, router_ref, gain_ref = whole
        before, qkv, context, middle, combine, slots = ([None] + list(outs))[-6:]
        hidden_rows = images[0][:rows]
        if mixing is not None:
            hidden_rows = hidden_rows + nn(images[1][:rows], images[2][...])
            before[:rows] = hidden_rows
        middle_rows = attention_forward(
            rows, limit, hidden_rows, gain_ref, attention_ref, qkv, context
        )
        middle[:rows] = middle_rows
        _, _, normed, dispatch, share = route(limit, middle_rows, gain_ref, router_ref)
        combine[:rows] = share.astype(BF16)
        slots[...] = tn(dispatch.astype(BF16), normed).astype(BF16)

    outs = [
        ((LEN, 3 * width), BF16),
        ((LEN, width), BF16),
        ((LEN, width), F32),
        ((LEN, experts), BF16),
        ((experts, width), BF16),
    ]
    if mixing is not None:
        outs = [((LEN, width), F32)] + outs
    return by_image(
        "sparse_forward",
        body,
        [resolution],
        [hidden] + list(mixing or ()),
        [attention, router, gains],
        outs,
        [],
    )


def top(resolution, labels, middle, combine, returned, head, head_bias, last_gains, classes, images, devices):
    width = middle.shape[2]
    experts = returned.shape[1]
    padded = head.shape[1]

    def body(rows, limit, numbers, per_image, whole, outs, sums, scratch):
        middle_ref, combine_ref, returned_ref = per_image
        head_ref, bias_ref, gain_ref = whole
        grad_hidden, grad_returned = outs
        grad_head, grad_bias_row, grad_gains, loss = sums
        length = float(LEN if limit is None else LEN_LO)
        share = combine_ref[:rows]
        hidden = middle_ref[:rows] + nn(share, returned_ref[...])
        unit, rate = normalise(hidden)
        normed = masked_rows(limit, unit * gain_ref[0:1] + gain_ref[1:2])
        pooled = jnp.sum(normed, 0, keepdims=True) * (1.0 / length)
        one_row = (row_number((8, width)) == 0).astype(F32)
        pooled_b = (one_row * pooled).astype(BF16)
        logits = nn(pooled_b, head_ref[...])[0:1] + bias_ref[...]
        shifted = logits - jnp.max(logits, 1, keepdims=True)
        raised = jnp.exp(shifted)
        total = jnp.sum(raised, 1, keepdims=True)
        log_probs = shifted - jnp.log(total)
        lane = lax.broadcasted_iota(jnp.int32, (1, padded), 1)
        target = jnp.where(lane == numbers[1], 1.0 - SMOOTH, 0.0) + jnp.where(
            lane < classes, SMOOTH / classes, 0.0
        )
        picked = jnp.sum(target * log_probs, 1, keepdims=True)
        loss[...] += jnp.broadcast_to(picked * (-1.0 / images), loss.shape)
        grad_logits = (raised * (1.0 / total) - target) * (1.0 / images)
        grad_bias_row[0:1] += grad_logits
        row_mask = (row_number((8, padded)) == 0).astype(F32)
        grad_logits_b = (row_mask * grad_logits).astype(BF16)
        grad_head[...] += tn(grad_logits_b, pooled_b)
        grad_pooled = nt(grad_logits_b, head_ref[...])[0:1] * (1.0 / length)
        grad_normed = masked_rows(limit, jnp.broadcast_to(grad_pooled, (rows, width)))
        grad_rows, grad_gain, grad_bias = normalise_back(
            unit, rate, gain_ref[0:1], grad_normed
        )
        grad_gains[0:1] += grad_gain
        grad_gains[1:2] += grad_bias
        grad_hidden[:rows] = grad_rows
        grad_returned[...] = tn(share, grad_rows.astype(BF16)).astype(BF16)

    return by_image(
        "top",
        body,
        [resolution, labels],
        [middle, combine, returned],
        [head, head_bias, last_gains],
        [((LEN, width), F32), ((experts, width), BF16)],
        [(padded, width), (8, padded), (8, width), (8, 128)],
        pack=devices
        and (
            1, devices, padded // devices,
            lambda sums, device: rows_of(sums[0], device, padded // devices),
        ),
    )


def sparse_backward(
    resolution, hidden, qkv, context, middle, grad_hidden, returned, grad_home, below, attention,
    router, gains, devices,
):
    width = middle.shape[2]
    experts = router.shape[0]
    chips = lax.axis_size("fsdp")
    local = experts // chips

    def body(rows, limit, numbers, images, whole, outs, sums, scratch):
        hidden_ref, qkv_ref, context_ref, middle_ref, grad_ref, returned_ref, home_ref = images[:7]
        attention_ref, router_ref, gain_ref = whole
        grad_attention, grad_router, grad_gains = sums
        grad = grad_ref[:rows]
        grad_combine = nt(grad.astype(BF16), returned_ref[...])
        unit, rate, normed, dispatch, share = route(
            limit, middle_ref[:rows], gain_ref, router_ref
        )
        home = home_ref[...]
        grad_dispatch = nt(normed, home)
        grad_normed = nn(dispatch.astype(BF16), home)
        grad_route = dispatch * (
            grad_dispatch - jnp.sum(grad_dispatch * dispatch, 0, keepdims=True)
        ) + share * (grad_combine - jnp.sum(grad_combine * share, 1, keepdims=True))
        grad_route_b = grad_route.astype(BF16)
        grad_router[...] += tn(grad_route_b, normed)
        grad_normed = grad_normed + nn(grad_route_b, router_ref[...])
        grad_in, grad_gain, grad_bias = normalise_back(unit, rate, gain_ref[2:3], grad_normed)
        grad_gains[2:3] += grad_gain
        grad_gains[3:4] += grad_bias
        grad_rows = attention_backward(
            rows, limit, hidden_ref[:rows], grad + grad_in, gain_ref, attention_ref, qkv_ref,
            context_ref, scratch[0], scratch[1], grad_attention, grad_gains,
        )
        outs[0][:rows] = grad_rows
        if below is not None:
            outs[1][...] = tn(images[7][:rows], grad_rows.astype(BF16)).astype(BF16)

    outs = [((LEN, width), F32)]
    if below is not None:
        outs.append(((experts, width), BF16))
    return by_image(
        "sparse_backward",
        body,
        [resolution],
        [hidden, qkv, context, middle, grad_hidden, returned, grad_home]
        + ([] if below is None else [below]),
        [attention, router, gains],
        outs,
        [(4 * width, width), (experts, width), (8, width)],
        [pltpu.VMEM((LEN, width), BF16), pltpu.VMEM((LEN, 3 * width), BF16)],
        pack=devices
        and (
            2, devices, up_16(4 * width // devices + local),
            lambda sums, device: padded_rows(
                [
                    rows_of(sums[0], device, 4 * width // devices),
                    rows_of(sums[1], device % chips, local),
                ]
            ),
        ),
    )


def first_backward(
    resolution, patches, start, qkv, context, middle, grad_hidden, dense, attention, gains, devices
):
    width = middle.shape[2]
    pixels = patches.shape[2]
    columns = dense.shape[0]

    def body(rows, limit, numbers, images, whole, outs, sums, scratch):
        patches_ref, start_ref, qkv_ref, context_ref, middle_ref, grad_ref = images
        dense_ref, attention_ref, gain_ref = whole
        grad_dense, grad_attention, grad_gains, grad_low, grad_high = sums
        grad_middle = mlp_backward(
            rows, middle_ref[:rows], grad_ref[:rows], gain_ref, dense_ref, pixels, grad_dense,
            grad_gains,
        )
        grad_rows = attention_backward(
            rows, limit, start_ref[:rows], grad_middle, gain_ref, attention_ref, qkv_ref,
            context_ref, scratch[0], scratch[1], grad_attention, grad_gains,
        )
        grad_rows = masked_rows(limit, grad_rows)
        grad_dense[:pixels] += tn(patches_ref[:rows], grad_rows.astype(BF16))
        if limit is None:
            grad_high[...] += grad_rows
        else:
            grad_low[...] += grad_rows

    return by_image(
        "first_backward",
        body,
        [resolution],
        [patches, start, qkv, context, middle, grad_hidden],
        [dense, attention, gains],
        [],
        [(columns, width), (4 * width, width), (8, width), (ROWS_LO, width), (LEN, width)],
        [pltpu.VMEM((LEN, width), BF16), pltpu.VMEM((LEN, 3 * width), BF16)],
        pack=devices
        and (
            2, devices, up_16((columns + 4 * width) // devices),
            lambda sums, device: padded_rows(
                [
                    rows_of(sums[0], device, columns // devices),
                    rows_of(sums[1], device, 4 * width // devices),
                ]
            ),
        ),
    )


def to_experts(values):
    return lax.all_to_all(values, "fsdp", split_axis=1, concat_axis=0, tiled=True)


def from_experts(values):
    return lax.all_to_all(values, "fsdp", split_axis=0, concat_axis=1, tiled=True)


def all_rows(values):
    return lax.all_gather(to_experts(values), "dp", axis=0, tiled=True).transpose(1, 0, 2)


def rows_home(part):
    shared = lax.psum_scatter(part.transpose(1, 0, 2), "dp", scatter_dimension=0, tiled=True)
    return from_experts(shared.astype(BF16))


def plain_exchange(layer, values, received, expert_in, expert_out):
    win, wout = expert_in[layer].astype(BF16), expert_out[layer].astype(BF16)
    rows = all_rows(values)
    if received is None:
        hid = gelu(matmul(rows, win, "end,edf->enf")).astype(BF16)
        return rows_home(matmul(hid, wout, "enf,efd->end")), rows
    hid, slope = gelu_both(matmul(received, win, "end,edf->enf"))
    hid = hid.astype(BF16)
    grad_pre = (matmul(rows, wout, "end,efd->enf") * slope).astype(BF16)
    home = rows_home(matmul(grad_pre, win, "enf,edf->end"))

    def gram(values):
        return matmul(values, values, "enk,emk->enm")

    squares = gram(received) * gram(grad_pre) + gram(hid) * gram(rows)
    return home, hid, grad_pre, rows, jnp.sum(squares, (0, 1)).reshape(1, -1)


def fetch_layer(attention_t, router_t):
    width = attention_t.shape[1]
    flat = router_t.reshape(-1)
    pack = jnp.concatenate(
        [attention_t, jnp.pad(flat, (0, -flat.size % width)).reshape(-1, width)], 0
    )
    return lax.all_gather(pack, ("dp", "fsdp"), axis=0)


def open_layer(both, part, part_cols, part_rows):
    width = both.shape[2]
    rows_dp = lax.axis_size("dp")
    cols_fsdp = lax.axis_size("fsdp")
    router = (
        both[:, part:]
        .reshape(rows_dp * cols_fsdp, -1)[:, : part_cols * part_rows]
        .reshape(rows_dp, cols_fsdp, part_cols, part_rows)
        .transpose(1, 2, 0, 3)
        .reshape(cols_fsdp * part_cols, rows_dp * part_rows)
    )
    return both[:, :part].reshape(-1, width), router


def share_layer(grad_attention, grad_router, part_cols, part_rows):
    rows_dp = lax.axis_size("dp")
    cols_fsdp = lax.axis_size("fsdp")
    devices = rows_dp * cols_fsdp
    width = grad_attention.shape[1]
    router = (
        grad_router.reshape(cols_fsdp, part_cols, rows_dp, part_rows)
        .transpose(2, 0, 1, 3)
        .reshape(devices, -1)
    )
    router = jnp.pad(router, ((0, 0), (0, -part_cols * part_rows % width)))
    router = router.reshape(devices, -1, width)
    pack = jnp.concatenate([grad_attention.reshape(devices, -1, width), router], 1)
    mine = lax.psum_scatter(pack, ("dp", "fsdp"), scatter_dimension=0, tiled=False)
    part = grad_attention.shape[0] // devices
    return mine[:part], mine[part:].reshape(-1)[: part_cols * part_rows].reshape(part_cols, part_rows)


BITS = 4
GATHER_ORDERS = ((3, 2, 0, 1), (0, 1, 2, 3), (0, 1, 3, 2))
MESH_IDS = pl.DeviceIdType.MESH


def my_bits():
    at = lax.axis_index("fsdp")
    return [(at // (1 << (BITS - 1 - bit))) % 2 for bit in range(BITS)]


def partner_of(bit):
    at = lax.axis_index("fsdp")
    step = 1 << (BITS - 1 - bit)
    return (lax.axis_index("dp"), at + step * (1 - 2 * ((at // step) % 2)))


def sibling():
    return (1 - lax.axis_index("dp"), lax.axis_index("fsdp"))


def greet_partners():
    barrier = pltpu.get_barrier_semaphore()
    others = [partner_of(bit) for bit in range(BITS)] + [sibling()]
    for other in others:
        pl.semaphore_signal(barrier, inc=1, device_id=other, device_id_type=MESH_IDS)
    pl.semaphore_wait(barrier, len(others))


def send(source, target, send_sem, recv_sem, device):
    copy = pltpu.make_async_remote_copy(
        src_ref=source,
        dst_ref=target,
        send_sem=send_sem,
        recv_sem=recv_sem,
        device_id=device,
        device_id_type=MESH_IDS,
    )
    copy.start()
    return copy


def spread(parts, sems):
    mine = my_bits()
    core = lax.axis_index("dp")
    to_send, to_get, pass_send, pass_get = sems

    def view(part, stage, other):
        ref, lane_part, order = part
        index = []
        for bit in range(BITS):
            if bit in order[:stage]:
                index.append(slice(None))
            elif other and bit == order[stage]:
                index.append(1 - mine[bit])
            else:
                index.append(mine[bit])
        return ref.at[(core, *index, slice(None), lane_part)]

    def go(number, stage):
        block = view(parts[number], stage, False)
        return send(
            block, block, to_send.at[number, stage], to_get.at[number, stage],
            partner_of(parts[number][2][stage]),
        )

    def hand_over(number, slot, block):
        return send(block, block, pass_send.at[number, slot], pass_get.at[number, slot], sibling())

    going = [go(number, 0) for number in range(len(parts))]
    handed = [
        hand_over(number, BITS, view(parts[number], 0, False)) for number in range(len(parts))
    ]
    for stage in range(BITS):
        for number in range(len(parts)):
            going[number].wait()
            if stage + 1 < BITS:
                going[number] = go(number, stage + 1)
            handed.append(hand_over(number, stage, view(parts[number], stage, True)))
    for copy in handed:
        copy.wait()


def spread_sems(count):
    return [pltpu.SemaphoreType.DMA((count, BITS + 1)) for _ in range(4)]


def lane_parts(width):
    return [slice(start, start + 128) for start in range(0, width, 128)]


def gather_all(shards, collective_id):
    count = len(shards)
    width = shards[0].shape[1]
    cuts = lane_parts(width)

    def kernel(*refs):
        ins, outs, sems = refs[:count], refs[count : 2 * count], refs[2 * count :]
        place = (lax.axis_index("dp"), *my_bits())
        for ref, out in zip(ins, outs):
            out[place] = ref[...]
        greet_partners()
        spread(
            [
                (out, cut, GATHER_ORDERS[number % 3])
                for number, cut in enumerate(cuts)
                for out in outs
            ],
            sems,
        )

    outs = pl.pallas_call(
        kernel,
        in_specs=[pl.BlockSpec(memory_space=pltpu.VMEM)] * count,
        out_specs=[pl.BlockSpec(memory_space=pltpu.VMEM)] * count,
        out_shape=[jax.ShapeDtypeStruct((2,) * (BITS + 1) + s.shape, s.dtype) for s in shards],
        scratch_shapes=spread_sems(count * len(cuts)),
        compiler_params=pltpu.CompilerParams(
            collective_id=collective_id, has_side_effects=True, vmem_limit_bytes=VMEM_BYTES
        ),
        cost_estimate=work_of(40),
        name="gather_all",
    )(*shards)
    return [out.reshape(-1, width) for out in outs]


def reduce_all(grads, stats, shared, halved, collective_id):
    width = grads[0].shape[2]
    count = len(grads)
    starts = [sum(grad.shape[1] for grad in grads[:at]) for at in range(count + 1)]
    rows = starts[-1]
    cuts = lane_parts(width)
    parts = len(cuts)
    orders = [tuple(reversed(GATHER_ORDERS[number % 3])) for number in range(parts)]

    def kernel(*refs):
        grads_refs = refs[:count]
        stats_ref, mine_ref, shared_ref, total_ref = refs[count : count + 4]
        scratch = refs[count + 4 :]
        sums, first_get = scratch[:2]
        gets = scratch[2 : 2 + BITS]
        stats_all = scratch[2 + BITS]
        local_sem, pair_send, pair_get, to_send, to_get = scratch[3 + BITS : 8 + BITS]
        sems = scratch[8 + BITS :]
        core = lax.axis_index("dp")
        bits = my_bits()
        places = [
            (number, at, cut, slice(starts[at], starts[at + 1]))
            for number, cut in enumerate(cuts)
            for at in range(count)
        ]
        local = {
            (number, at): pltpu.make_async_copy(
                grads_refs[at].at[core, :, :, :, :, :, cut],
                sums.at[:, :, :, :, span, cut],
                local_sem.at[number, at],
            )
            for number, at, cut, span in places
        }
        for copy in local.values():
            copy.start()
        greet_partners()
        pairs = {
            (number, at): send(
                grads_refs[at].at[1 - core, :, :, :, :, :, cut],
                first_get.at[:, :, :, :, span, cut],
                pair_send.at[number, at],
                pair_get.at[number, at],
                sibling(),
            )
            for number, at, cut, span in places
        }

        def index(number, stage, own):
            order = orders[number]
            found = []
            for bit in range(BITS):
                if bit in order[:stage]:
                    found.append(bits[bit])
                elif bit == order[stage]:
                    found.append(bits[bit] if own else 1 - bits[bit])
                else:
                    found.append(slice(None))
            return (*found, slice(None), cuts[number])

        def go(number, stage):
            return send(
                sums.at[index(number, stage, False)],
                gets[stage].at[number],
                to_send.at[number, stage],
                to_get.at[number, stage],
                partner_of(orders[number][stage]),
            )

        going = [None] * parts
        turns = [number for number in range(parts) if number % 3] + list(range(0, parts, 3))
        for number in reversed(turns):
            for at in range(count):
                local[number, at].wait()
                pairs[number, at].wait()
            whole = (slice(None),) * (BITS + 1) + (cuts[number],)
            sums[whole] = sums[whole] + first_get[whole]
            going[number] = go(number, 0)
        place = tuple(bits)
        for stage in range(BITS):
            for number in turns:
                going[number].wait()
                if stage + 1 < BITS:
                    at = index(number, stage, True)
                    sums[at] = sums[at] + gets[stage][number]
                    going[number] = go(number, stage + 1)
                else:
                    at = index(number, stage, True)
                    mine_ref[:, cuts[number]] = sums[at].astype(F32) + gets[stage][number].astype(F32)
        mine = mine_ref[...]
        row = row_number((rows, width))
        counted = mine * mine
        for low, high in halved:
            counted = jnp.where((row >= low) & (row < high), 0.5 * counted, counted)
        squares = jnp.sum(jnp.sum(counted, 0, keepdims=True), 1, keepdims=True)
        top_row = (row_number((8, 128)) == 0).astype(F32)
        stats_all[(core, *place)] = stats_ref[...] + top_row * squares
        shared_ref[(core, *place)] = mine_ref[rows - shared :, :].astype(BF16)
        spread(
            [
                (shared_ref, cut, GATHER_ORDERS[number % 3]) for number, cut in enumerate(cuts)
            ]
            + [(stats_all, slice(0, 128), GATHER_ORDERS[1])],
            sems,
        )
        total_ref[...] = jnp.sum(stats_all[...].reshape(32, 8, 128), 0)

    grid = (2,) * BITS
    return pl.pallas_call(
        kernel,
        in_specs=[pl.BlockSpec(memory_space=pl.ANY)] * count
        + [pl.BlockSpec(memory_space=pltpu.VMEM)],
        out_specs=[pl.BlockSpec(memory_space=pltpu.VMEM)] * 3,
        out_shape=[
            jax.ShapeDtypeStruct((rows, width), F32),
            jax.ShapeDtypeStruct((2,) + grid + (shared, width), BF16),
            jax.ShapeDtypeStruct((8, 128), F32),
        ],
        scratch_shapes=[pltpu.VMEM(grid + (rows, width), BF16)] * 2
        + [pltpu.VMEM((parts,) + (2,) * (BITS - 1 - stage) + (rows, 128), BF16) for stage in range(BITS)]
        + [pltpu.VMEM((2,) + grid + (8, 128), F32)]
        + [pltpu.SemaphoreType.DMA((parts, count))] * 3
        + [pltpu.SemaphoreType.DMA((parts, BITS))] * 2
        + spread_sems(parts + 1),
        compiler_params=pltpu.CompilerParams(
            collective_id=collective_id, has_side_effects=True, vmem_limit_bytes=VMEM_BYTES
        ),
        cost_estimate=work_of(60),
        name="reduce_all",
    )(*[grad.reshape((2,) + grid + grad.shape[1:]) for grad in grads], stats)


def chip(at):
    return (lax.axis_index("dp"), at)


def greet_all(chips):
    barrier = pltpu.get_barrier_semaphore()
    me = lax.axis_index("fsdp")

    def one(step, carry):
        pl.semaphore_signal(
            barrier, inc=1, device_id=chip((me + step) % chips), device_id_type=MESH_IDS
        )
        return carry

    lax.fori_loop(1, chips, one, 0)
    pl.semaphore_signal(barrier, inc=1, device_id=sibling(), device_id_type=MESH_IDS)
    pl.semaphore_wait(barrier, chips)


def swap_start(chips, source, target, send_sem, get_sem):
    me = lax.axis_index("fsdp")

    def one(step, carry):
        other = (me + step) % chips
        send(source.at[other], target.at[me], send_sem.at[other], get_sem.at[me], chip(other))
        return carry

    lax.fori_loop(1, chips, one, 0)


def swap_sent(chips, step, source, target, send_sem, get_sem):
    me = lax.axis_index("fsdp")
    to = (me + step) % chips
    pltpu.make_async_remote_copy(
        src_ref=source.at[to], dst_ref=target.at[me], send_sem=send_sem.at[to],
        recv_sem=get_sem.at[me], device_id=chip(to), device_id_type=MESH_IDS,
    ).wait_send()


def swap_arrived(chips, step, source, target, send_sem, get_sem):
    origin = (lax.axis_index("fsdp") + chips - step) % chips
    pltpu.make_async_remote_copy(
        src_ref=source.at[origin], dst_ref=target.at[origin], send_sem=send_sem.at[origin],
        recv_sem=get_sem.at[origin], device_id=chip(origin), device_id_type=MESH_IDS,
    ).wait_recv()
    return origin


def exchange(layer, values, received, expert_in, expert_out, collective_id):
    images, experts, width = values.shape
    chips = lax.axis_size("fsdp")
    cores = lax.axis_size("dp")
    local, _, hidden = expert_in.shape[1:]
    rows = images * local
    half = chips * images
    every = cores * half
    backward = received is not None

    def kernel(*refs):
        if backward:
            values_ref, received_ref, in_ref, out_ref = refs[:4]
            home_ref, hid_ref, pre_ref, gout_ref, squares_ref = refs[4:9]
            slope_ref = refs[9]
            scratch = refs[10:]
        else:
            values_ref, in_ref, out_ref = refs[:3]
            home_ref, received_ref = refs[3:5]
            scratch = refs[5:]
        win, wout, outbox, inbox, parts, pair_out, pair_in, sorted_ref, backbox, homebox = scratch[:10]
        win_sem, wout_sem, send_one, get_one, pass_send, pass_get, pair_send, pair_get, send_two, get_two = scratch[10:]
        core = lax.axis_index("dp")
        me = lax.axis_index("fsdp")

        def fetch(e):
            return (
                pltpu.make_async_copy(in_ref.at[layer, e], win.at[e], win_sem.at[e]),
                pltpu.make_async_copy(out_ref.at[layer, e], wout.at[e], wout_sem.at[e]),
            )

        def start_fetch(e, carry):
            for copy in fetch(e):
                copy.start()
            return carry

        lax.fori_loop(0, local, start_fetch, 0)
        whole = [values_ref[image].astype(F32) for image in range(images)]
        for at in range(chips):
            outbox[at] = jnp.concatenate(
                [one[at * local : (at + 1) * local] for one in whole], 0
            ).astype(BF16)
        greet_all(chips)
        swap_start(chips, outbox, inbox.at[core], send_one, get_one)
        inbox[core, me] = outbox[me]

        def hand(at):
            block = inbox.at[core, at]
            return pltpu.make_async_remote_copy(
                src_ref=block, dst_ref=block, send_sem=pass_send.at[at],
                recv_sem=pass_get.at[at], device_id=sibling(), device_id_type=MESH_IDS,
            )

        def handed(at):
            block = inbox.at[1 - core, at]
            return pltpu.make_async_remote_copy(
                src_ref=block, dst_ref=block, send_sem=pass_send.at[at],
                recv_sem=pass_get.at[at], device_id=sibling(), device_id_type=MESH_IDS,
            )

        hand(me).start()
        if backward:

            def ahead(e, carry):
                for copy in fetch(e):
                    copy.wait()
                rec = received_ref[e]
                hid, slope = gelu_both(nn(rec, win[e].astype(BF16)))
                slope_ref[e] = slope
                hid_ref[e] = hid.astype(BF16)
                return carry

            lax.fori_loop(0, local, ahead, 0)

        def arrive(step, carry):
            hand(swap_arrived(chips, step, outbox, inbox.at[core], send_one, get_one)).start()
            return carry

        lax.fori_loop(1, chips, arrive, 0)

        def all_handed(at, carry):
            handed(at).wait_recv()
            return carry

        lax.fori_loop(0, chips, all_handed, 0)
        arrived = inbox[...].reshape(every * local, width)
        pick_row = lax.broadcasted_iota(jnp.int32, (every, every * local), 0)
        pick_col = lax.broadcasted_iota(jnp.int32, (every, every * local), 1)
        wanted = pick_row * local - pick_col

        def pair_copy(e):
            return pltpu.make_async_remote_copy(
                src_ref=pair_out.at[e], dst_ref=pair_in.at[e], send_sem=pair_send.at[e],
                recv_sem=pair_get.at[e], device_id=sibling(), device_id_type=MESH_IDS,
            )

        if backward:
            squares_ref[...] = jnp.zeros_like(squares_ref)

        def work(e, carry):
            pick = (wanted == -e).astype(F32).astype(BF16)
            mine = nn(pick, arrived).astype(BF16)
            if backward:
                gout_ref[e] = mine
                grad_pre = (nt(mine, wout[e].astype(BF16)) * slope_ref[e]).astype(BF16)
                pre_ref[e] = grad_pre
                part = nt(grad_pre, win[e].astype(BF16))
                rec, hid = received_ref[e], hid_ref[e]
                product = nt(rec, rec) * nt(grad_pre, grad_pre) + nt(hid, hid) * nt(mine, mine)
                squares_ref[...] += jnp.sum(product.reshape(every // 8, 8, every), 0)
            else:
                for copy in fetch(e):
                    copy.wait()
                received_ref[e] = mine
                hid = gelu(nn(mine, win[e].astype(BF16))).astype(BF16)
                part = nn(hid, wout[e].astype(BF16))
            parts[e] = part.reshape(cores, half, width)
            pair_out[e] = parts[e, 1 - core].astype(BF16)
            pair_copy(e).start()
            return carry

        lax.fori_loop(0, local, work, 0)

        def add(e, carry):
            pair_copy(e).wait_recv()
            sorted_ref[pl.ds(pl.multiple_of(e * half, half), half)] = (
                parts[e, core] + pair_in[e].astype(F32)
            ).astype(BF16)
            return carry

        lax.fori_loop(0, local, add, 0)
        back_row = lax.broadcasted_iota(jnp.int32, (half * local, half * local), 0)
        back_col = lax.broadcasted_iota(jnp.int32, (half * local, half * local), 1)
        back = (back_row == (back_col % half) * local + back_col // half).astype(F32).astype(BF16)
        backbox[...] = nn(back, sorted_ref[...]).astype(BF16).reshape(chips, rows, width)
        swap_start(chips, backbox, homebox, send_two, get_two)
        homebox[me] = backbox[me]

        def home(step, carry):
            swap_arrived(chips, step, backbox, homebox, send_two, get_two)
            return carry

        lax.fori_loop(1, chips, home, 0)
        blocks = [homebox[at].astype(F32) for at in range(chips)]
        for image in range(images):
            home_ref[image] = jnp.concatenate(
                [block[image * local : (image + 1) * local] for block in blocks], 0
            ).astype(BF16)

        def drain(step, carry):
            swap_sent(chips, step, outbox, inbox.at[core], send_one, get_one)
            swap_sent(chips, step, backbox, homebox, send_two, get_two)
            return carry

        lax.fori_loop(1, chips, drain, 0)

        def drain_pass(at, carry):
            hand(at).wait_send()
            return carry

        lax.fori_loop(0, chips, drain_pass, 0)

        def drain_pair(e, carry):
            pair_copy(e).wait_send()
            return carry

        lax.fori_loop(0, local, drain_pair, 0)

    inside = pl.BlockSpec(memory_space=pltpu.VMEM)
    outside = pl.BlockSpec(memory_space=pl.ANY)
    shape = jax.ShapeDtypeStruct
    home_shape = shape((images, experts, width), BF16)
    if backward:
        out_shape = [
            home_shape,
            shape((local, every, hidden), BF16),
            shape((local, every, hidden), BF16),
            shape((local, every, width), BF16),
            shape((8, every), F32),
        ]
        operands = (values, received, expert_in, expert_out)
        in_specs = [inside, inside, outside, outside]
        extra = [pltpu.VMEM((local, every, hidden), F32)]
    else:
        out_shape = [home_shape, shape((local, every, width), BF16)]
        operands = (values, expert_in, expert_out)
        in_specs = [inside, outside, outside]
        extra = []
    dma = pltpu.SemaphoreType.DMA
    return pl.pallas_call(
        kernel,
        in_specs=in_specs,
        out_specs=[inside] * len(out_shape),
        out_shape=out_shape,
        scratch_shapes=extra
        + [
            pltpu.VMEM((local, width, hidden), F32),
            pltpu.VMEM((local, hidden, width), F32),
            pltpu.VMEM((chips, rows, width), BF16),
            pltpu.VMEM((cores, chips, rows, width), BF16),
            pltpu.VMEM((local, cores, half, width), F32),
            pltpu.VMEM((local, half, width), BF16),
            pltpu.VMEM((local, half, width), BF16),
            pltpu.VMEM((local * half, width), BF16),
            pltpu.VMEM((chips, rows, width), BF16),
            pltpu.VMEM((chips, rows, width), BF16),
        ]
        + [dma((local,))] * 2
        + [dma((chips,))] * 4
        + [dma((local,))] * 2
        + [dma((chips,))] * 2,
        compiler_params=pltpu.CompilerParams(
            collective_id=collective_id, has_side_effects=True, vmem_limit_bytes=VMEM_BYTES
        ),
        cost_estimate=work_of(40),
        name="exchange_back" if backward else "exchange",
    )(*operands)


def expert_adam(weight, first, second, lefts, rights, scale, rate):
    layers, local, tall, wide = weight.shape
    deep = lefts[0].shape[1]
    each = 2 if local % 2 == 0 else 1

    def kernel(scale_ref, w_ref, m_ref, s_ref, *refs):
        left_refs, right_refs = refs[:layers], refs[layers : 2 * layers]
        new_w, new_m, new_s = refs[2 * layers :]

        for layer in range(layers):

            @pl.when(pl.program_id(0) == layer)
            def _(layer=layer):
                for e in range(each):
                    grad = tn(left_refs[layer][e], right_refs[layer][e]) * scale_ref[0]
                    moment = BETA_ONE * m_ref[e] + (1.0 - BETA_ONE) * grad
                    spread_of = BETA_TWO * s_ref[e] + (1.0 - BETA_TWO) * (grad * grad)
                    ratio = (moment * (1.0 / (1.0 - BETA_ONE**STEP))) / (
                        jnp.sqrt(spread_of * (1.0 / (1.0 - BETA_TWO**STEP))) + ADAM_EPS
                    )
                    held = w_ref[e]
                    new_m[e] = moment
                    new_s[e] = spread_of
                    new_w[e] = held - rate * (ratio + WEIGHT_DECAY * held)

    def factor_spec(layer, columns):
        last = local // each - 1
        return pl.BlockSpec(
            (each, deep, columns),
            lambda l, e: (jnp.where(l == layer, e, jnp.where(l < layer, 0, last)), 0, 0),
        )

    block = pl.BlockSpec((None, each, tall, wide), lambda l, e: (l, e, 0, 0))
    return pl.pallas_call(
        kernel,
        grid=(layers, local // each),
        in_specs=[pl.BlockSpec(memory_space=pltpu.SMEM)]
        + [block] * 3
        + [factor_spec(layer, tall) for layer in range(layers)]
        + [factor_spec(layer, wide) for layer in range(layers)],
        out_specs=[block] * 3,
        out_shape=[jax.ShapeDtypeStruct(weight.shape, F32)] * 3,
        compiler_params=pltpu.CompilerParams(vmem_limit_bytes=VMEM_BYTES),
        name="expert_adam",
    )(scale, weight, first, second, *lefts, *rights)


def level_pair(patches, resolution, labels):
    swap = [(0, 1), (1, 0)]
    images = resolution.shape[0]
    place = jnp.arange(images, dtype=jnp.int32)
    count = jnp.sum(resolution)
    other = lax.ppermute(count, "dp", swap)
    moves = jnp.abs(count - other) >= 2
    wanted = (count > other).astype(jnp.int32)
    at = jnp.min(jnp.where(resolution == wanted, place, images - 1))
    chosen = place == at
    out = lax.dynamic_slice_in_dim(patches, at, 1, 0)
    got = lax.ppermute(out, "dp", swap)
    label = lax.ppermute(jnp.sum(jnp.where(chosen, labels, 0)), "dp", swap)
    patches = lax.dynamic_update_slice_in_dim(patches, jnp.where(moves, got, out), at, 0)
    moved = chosen & moves
    return (
        patches,
        jnp.where(moved, 1 - resolution, resolution),
        jnp.where(moved, label, labels),
    )


def adam(weight, first, second, grad, rate):
    first = BETA_ONE * first + (1.0 - BETA_ONE) * grad
    second = BETA_TWO * second + (1.0 - BETA_TWO) * grad * grad
    ratio = first / (1.0 - BETA_ONE**STEP) / (jnp.sqrt(second / (1.0 - BETA_TWO**STEP)) + ADAM_EPS)
    return (weight - rate * (ratio + WEIGHT_DECAY * weight), first, second)


def on_device(
    patches,
    resolution,
    labels,
    dense_weights,
    attention,
    router,
    expert_in,
    expert_out,
    classifier,
    norm_table,
    dense_weights_first,
    dense_weights_second,
    attention_first,
    attention_second,
    router_first,
    router_second,
    expert_in_first,
    expert_in_second,
    expert_out_first,
    expert_out_second,
    classifier_first,
    classifier_second,
    norm_table_first,
    norm_table_second,
):
    layers = attention.shape[0]
    width = norm_table.shape[1]
    classes = classifier.shape[1]
    devices = lax.axis_size("dp") * lax.axis_size("fsdp")
    images = patches.shape[0] * devices
    interp = interp_matrix()
    position = norm_table[:LEN_LO]
    pos_high = jnp.dot(interp, position, precision=PRECISE)
    pos_low = jnp.pad(position, ((0, LEN - LEN_LO), (0, 0)))
    positions = jnp.stack([pos_low, pos_high])
    gains = [
        jnp.pad(norm_table[LEN_LO + 4 * layer : LEN_LO + 4 * layer + 4], ((0, 4), (0, 0)))
        for layer in range(layers)
    ]
    last_gains = jnp.pad(norm_table[LEN_LO + 4 * layers :], ((0, 6), (0, 0)))
    attention_t = attention.transpose(0, 2, 1).astype(BF16)
    router_t = router.transpose(0, 2, 1).astype(BF16)
    dense_t = dense_weights.T.astype(BF16)
    local = expert_in.shape[1]
    own = (
        lax.axis_size("dp") == 2
        and lax.axis_size("fsdp") == 1 << BITS
        and patches.shape[0] * local % 16 == 0
        and router.shape[1] * router.shape[2] % width == 0
    )
    if own:
        patches, resolution, labels = level_pair(patches, resolution, labels)
        dense, attention_one = gather_all([dense_t, attention_t[0]], 0)
    else:
        dense, attention_one = [
            lax.all_gather(part, ("dp", "fsdp"), axis=0, tiled=True)
            for part in (dense_t, attention_t[0])
        ]
    attention_all = [attention_one]
    router_all = [None]
    fetched = [None]
    for layer in range(1, layers):
        share = attention_t[layer]
        if layer > 1:
            share, attention_all[0] = lax.optimization_barrier((share, attention_all[0]))
        fetched.append(fetch_layer(share, router_t[layer - 1]))

    start, qkv, context, middle, hidden = first_forward(
        resolution, patches, dense, attention_all[0], positions, gains[0], width
    )
    kept = [(start, qkv, context, middle)]
    mixing = None
    for layer in range(1, layers):
        both = fetched[layer]
        if mixing is not None:
            both, last = lax.optimization_barrier((both, mixing[1]))
            mixing = (mixing[0], last)
        one, two = open_layer(both, attention_t.shape[1], router.shape[2], router.shape[1])
        attention_all.append(one)
        router_all.append(two)
        outs = sparse_forward(
            resolution, hidden, mixing, attention_all[layer], router_all[layer], gains[layer]
        )
        if mixing is not None:
            hidden = outs[0]
        qkv, context, middle, combine, slots = outs[-5:]
        if own:
            returned, received = exchange(layer - 1, slots, None, expert_in, expert_out, layer)
        else:
            returned, received = plain_exchange(layer - 1, slots, None, expert_in, expert_out)
        kept.append((hidden, qkv, context, middle, combine, returned, received))
        hidden = middle
        mixing = (combine, returned)

    packs = devices if own else None
    padding = -classes % 128 if not own else -classes % (16 * devices)
    head = jnp.pad(classifier[:width].astype(BF16), ((0, 0), (0, padding)))
    head_bias = jnp.pad(classifier[width:], ((0, 0), (0, padding)), constant_values=NEG_FILL)
    grad_hidden, grad_returned, grad_head, grad_bias, grad_last, loss_part = top(
        resolution, labels, middle, combine, returned, head, head_bias, last_gains, classes, images,
        packs,
    )
    attention_grads = [None] * layers
    router_grads = [None] * (layers - 1)
    gain_grads = [None] * layers
    layer_packs = [None] * layers
    in_factors = [None] * (layers - 1)
    out_factors = [None] * (layers - 1)
    local_squares = 0.0
    for layer in reversed(range(1, layers)):
        before, qkv, context, middle, combine, returned, received = kept[layer]
        if own:
            outs = exchange(
                layer - 1, grad_returned, received, expert_in, expert_out, layers + layer
            )
        else:
            outs = plain_exchange(layer - 1, grad_returned, received, expert_in, expert_out)
        grad_home, hid, grad_pre, grad_out, squares = outs
        local_squares = local_squares + jnp.sum(squares)
        in_factors[layer - 1] = (received, grad_pre)
        out_factors[layer - 1] = (hid, grad_out)
        below = kept[layer - 1][4] if layer > 1 else None
        outs = sparse_backward(
            resolution, before, qkv, context, middle, grad_hidden, returned, grad_home, below,
            attention_all[layer], router_all[layer], gains[layer], packs,
        )
        grad_hidden = outs[0]
        if below is not None:
            grad_returned = outs[1]
        grad_gain = outs[-1]
        if own:
            layer_packs[layer] = outs[-2]
        else:
            attention_grads[layer], router_grads[layer - 1] = outs[-3:-1]
        gain_grads[layer] = grad_gain[:4]
    start, qkv, context, middle = kept[0]
    outs = first_backward(
        resolution, patches, start, qkv, context, middle, grad_hidden, dense, attention_all[0],
        gains[0], packs,
    )
    grad_gain, grad_low, grad_high = outs[-3:]
    if own:
        layer_packs[0] = outs[0]
    else:
        grad_dense, attention_grads[0] = outs[:2]
    gain_grads[0] = grad_gain[:4]
    grad_pos = grad_low[:LEN_LO] + jnp.dot(interp.T, grad_high, precision=PRECISE)
    grad_table = jnp.concatenate([grad_pos] + gain_grads + [grad_last[:2]], 0)
    loss_local = loss_part[0, 0]
    part_rows, part_cols = router.shape[1:]
    table_rows = grad_table.shape[0]
    if own:
        bias_flat = grad_bias[0]
        bias_flat = jnp.pad(bias_flat, (0, -bias_flat.shape[0] % width)).reshape(-1, width)
        tail = jnp.concatenate([grad_table, bias_flat], 0).astype(BF16)
        tail = jnp.pad(tail, ((0, -tail.shape[0] % devices), (0, 0))).reshape(devices, -1, width)
        tail_each = tail.shape[1]
        tail = jnp.pad(tail, ((0, 0), (0, -tail_each % 16), (0, 0)))
        stats = jnp.concatenate(
            [
                jnp.broadcast_to(local_squares, (1, 128)),
                jnp.broadcast_to(loss_local, (1, 128)),
                jnp.zeros((6, 128), F32),
            ],
            0,
        )
        blocks = layer_packs + [grad_head, tail]
        starts = [sum(block.shape[1] for block in blocks[:at]) for at in range(layers)]
        columns = dense.shape[0] // devices
        part = attention_t.shape[1]
        router_at = [starts[layer] + part for layer in range(1, layers)]
        mine, shared, totals = reduce_all(
            blocks, stats, grad_head.shape[1] + tail.shape[1],
            [(at, at + part_cols) for at in router_at], 2 * layers,
        )
        shared = shared.reshape(devices, -1, width)
        head_each = grad_head.shape[1]
        head_all = shared[:, :head_each].reshape(-1, width)[:classes].T.astype(F32)
        tail_all = shared[:, head_each : head_each + tail_each].reshape(-1, width).astype(F32)
        shared_table = tail_all[:table_rows]
        bias_all = tail_all[table_rows:].reshape(-1)[None, :classes]
        shared_head = jnp.concatenate([head_all, bias_all], 0)
        norm = jnp.sqrt(totals[0, 0])
        loss_total = totals[1, 0]
        grad_first = mine[:columns].T
        attention_at = [columns] + starts[1:]
        grad_attention = jnp.stack([mine[at : at + part].T for at in attention_at])
        lane_at = lax.axis_index("dp") * part_rows
        grad_router_all = jnp.stack(
            [
                lax.dynamic_slice_in_dim(mine[at : at + part_cols], lane_at, part_rows, 1).T
                for at in router_at
            ]
        )
    else:
        grad_first = lax.psum_scatter(
            grad_dense, ("dp", "fsdp"), scatter_dimension=0, tiled=True
        ).T
        shares = [
            share_layer(attention_grads[layer], router_grads[layer - 1], part_cols, part_rows)
            for layer in range(1, layers)
        ]
        first_share = lax.psum_scatter(
            attention_grads[0], ("dp", "fsdp"), scatter_dimension=0, tiled=True
        )
        grad_attention = jnp.stack([first_share] + [share[0] for share in shares])
        grad_attention = grad_attention.transpose(0, 2, 1)
        grad_router_all = jnp.stack([share[1] for share in shares]).transpose(0, 2, 1)
        local_squares = (
            local_squares
            + jnp.sum(grad_first * grad_first)
            + jnp.sum(grad_attention * grad_attention)
            + jnp.sum(grad_router_all * grad_router_all)
        )
        grad_head = jnp.concatenate([grad_head[:classes].T, grad_bias[0:1, :classes]], 0)
        shared_head, shared_table, loss_total, squares = lax.psum(
            (grad_head, grad_table, loss_local, local_squares), ("dp", "fsdp")
        )
        norm = jnp.sqrt(
            squares + jnp.sum(shared_head * shared_head) + jnp.sum(shared_table * shared_table)
        )
    scale = jnp.minimum(1.0, CLIP_NORM / norm)
    scale_row = scale.reshape(1)

    def experts_updated(weight, first, second, factors, rate):
        lefts, rights = zip(*factors)
        return tuple(expert_adam(weight, first, second, lefts, rights, scale_row, rate))

    updates = (
        adam(dense_weights, dense_weights_first, dense_weights_second, grad_first * scale, LEARN_RATE),
        adam(attention, attention_first, attention_second, grad_attention * scale, ATTENTION_RATE),
        adam(router, router_first, router_second, grad_router_all * scale, LEARN_RATE),
        experts_updated(expert_in, expert_in_first, expert_in_second, in_factors, EXPERT_RATE),
        experts_updated(expert_out, expert_out_first, expert_out_second, out_factors, LEARN_RATE),
        adam(classifier, classifier_first, classifier_second, shared_head * scale, LEARN_RATE),
        adam(norm_table, norm_table_first, norm_table_second, shared_table * scale, TABLE_RATE),
    )
    return (loss_total, norm) + tuple(part for update in updates for part in update)


def solution(mesh):
    spread = P(("dp", "fsdp"))
    weights = (
        P(None, ("dp", "fsdp")),
        P(None, None, ("dp", "fsdp")),
        P(None, "dp", "fsdp"),
        P(None, "fsdp", None, "dp"),
        P(None, "fsdp", "dp", None),
        P(),
        P(),
    )
    moments = tuple(spec for spec in weights for _ in range(2))
    triples = tuple(spec for spec in weights for _ in range(3))
    return jax.shard_map(
        on_device,
        mesh=mesh,
        in_specs=(spread, spread, spread) + weights + moments,
        out_specs=(P(), P()) + triples,
        check_vma=False,
    )
```

profile of v0, /device:TPU:0, one launch (start us, length us, event | category | flops | bytes accessed | tf_op | source)
XLA Modules:
  0.0 656.5 jit_solution(17745773617321667138)
XLA Ops:
  7.3 4.1 copy.89
  14.6 37.3 %gather_all.1 = (bf16[2,2,2,2,2,120,384]{6,5,4,3,2,1,0:T(8,128)(2,1)}, bf16[2,2,2,2,2,48,384]{6,5,4,3,2,1,0:T(8,128)(2,1)}) custom-call(bf16[120,384]{1,0:T(8,128)(2,1)} %convert_bitcast_fusion.2.refs_0_, bf16[48,384]{1,0:T(8,128)(2,1)} %get-tuple-element.241.refs_1_), custom_call_target="tpu_custom_call" | custom-call | flops 40000000000 | bytes 1048576 | tf_op jit(solution)/shard_map/gather_all/pallas_call | solution.py:787
  56.9 2.3 constant_dynamic-slice_fusion
  75.9 2.3 select_dynamic-update-slice_fusion.refs_1_
  78.2 24.7 %first_forward.1 = (f32[4,576,384]{2,1,0:T(8,128)}, bf16[4,576,1152]{2,1,0:T(8,128)(2,1)}, bf16[4,576,384]{2,1,0:T(8,128)(2,1)}, f32[4,576,384]{2,1,0:T(8,128)}, f32[4,576,384]{2,1,0:T(8,128)}) custom-call(s32[4]{0:T(128)} %and_select_fusion.1.refs_0_, bf16[4,576,768]{2,1,0:T(8,128)(2,1)} %select_dynamic-update-slice_fusion.refs_1_, ...), custom_call_target="tpu_custom_call" | custom-call | flops 32000000000 | bytes 1048576 | tf_op jit(solution)/shard_map/first_forward/pallas_call | solution.py:322
  104.8 2.4 slice.160
  107.2 16.3 %sparse_forward.2 = (bf16[4,576,1152]{2,1,0:T(8,128)(2,1)}, bf16[4,576,384]{2,1,0:T(8,128)(2,1)}, f32[4,576,384]{2,1,0:T(8,128)}, bf16[4,576,128]{2,1,0:T(8,128)(2,1)}, bf16[4,128,384]{2,1,0:T(8,128)(2,1)}) custom-call(s32[4]{0:T(128)} %and_select_fusion.1.refs_0_, f32[4,576,384]{2,1,0:T(8,128)} %get-tuple-element.92.refs_1_, bf16[1536,384]{1,0:T(8,128)(2,1)} %bitcast.82, ...), custom_call_target="tpu_custom_call" | custom-call | flops 32000000000 | bytes 1048576 | tf_op jit(solution)/shard_map/sparse_forward/pallas_call | solution.py:322
  123.6 40.9 %exchange.2 = (bf16[4,128,384]{2,1,0:T(8,128)(2,1)}, bf16[8,128,384]{2,1,0:T(8,128)(2,1)}) custom-call(bf16[4,128,384]{2,1,0:T(8,128)(2,1)} %get-tuple-element.98.refs_0_, f32[2,8,384,768]{3,2,1,0:T(8,128)} %w_ref.2, f32[2,8,768,384]{3,2,1,0:T(8,128)} %w_ref.3), custom_call_target="tpu_custom_call" | custom-call | flops 40000000000 | bytes 1048576 | tf_op jit(solution)/shard_map/exchange/pallas_call | solution.py:1170
  164.5 2.4 slice.129
  168.9 17.1 %sparse_forward.3 = (f32[4,576,384]{2,1,0:T(8,128)}, bf16[4,576,1152]{2,1,0:T(8,128)(2,1)}, bf16[4,576,384]{2,1,0:T(8,128)(2,1)}, f32[4,576,384]{2,1,0:T(8,128)}...) custom-call(s32[4]{0:T(128)} %and_select_fusion.1.refs_0_, ...), custom_call_target="tpu_custom_call" | custom-call | flops 32000000000 | bytes 1048576 | tf_op jit(solution)/shard_map/sparse_forward/pallas_call | solution.py:322
  186.0 39.3 %exchange.3 = (bf16[4,128,384]{2,1,0:T(8,128)(2,1)}, bf16[8,128,384]{2,1,0:T(8,128)(2,1)}) custom-call(bf16[4,128,384]{2,1,0:T(8,128)(2,1)} %get-tuple-element.107.refs_0_, f32[2,8,384,768]{3,2,1,0:T(8,128)} %w_ref.2, f32[2,8,768,384]{3,2,1,0:T(8,128)} %w_ref.3), custom_call_target="tpu_custom_call" | custom-call | flops 40000000000 | bytes 1048576 | tf_op jit(solution)/shard_map/exchange/pallas_call | solution.py:1170
  225.3 11.1 %top.1 = (f32[4,576,384]{2,1,0:T(8,128)}, bf16[4,128,384]{2,1,0:T(8,128)(2,1)}, bf16[32,32,384]{2,1,0:T(8,128)(2,1)}, f32[8,1024]{1,0:T(8,128)}, f32[8,384]{1,0:T(8,128)}, /*index=5*/f32[8,128]{1,0:T(8,128)}) custom-call(s32[4]{0:T(128)} %and_select_fusion.1.refs_0_, s32[4]{0:T(128)} %and_select_fusion.refs_1_, ...), custom_call_target="tpu_custom_call" | custom-call | flops 32000000000 | bytes 1048576 | tf_op jit(solution)/shard_map/top/pallas_call | solution.py:322
  236.4 38.1 %exchange_back.2 = (bf16[4,128,384]{2,1,0:T(8,128)(2,1)}, bf16[8,128,768]{2,1,0:T(8,128)(2,1)}, bf16[8,128,768]{2,1,0:T(8,128)(2,1)}, bf16[8,128,384]{2,1,0:T(8,128)(2,1)}, f32[8,128]{1,0:T(8,128)}) custom-call(bf16[4,128,384]{2,1,0:T(8,128)(2,1)} %get-tuple-element.110.refs_0_, bf16[8,128,384]{2,1,0:T(8,128)(2,1)} %get-tuple-element.111.refs_1_, ...), custom_call_target="tpu_custom_call" | custom-call | flops 40000000000 | bytes 1048576 | tf_op jit(solution)/shard_map/exchange_back/pallas_call | solution.py:1170
  274.5 31.1 %sparse_backward.2 = (f32[4,576,384]{2,1,0:T(8,128)}, bf16[4,128,384]{2,1,0:T(8,128)(2,1)}, bf16[32,64,384]{2,1,0:T(8,128)(2,1)}, f32[8,384]{1,0:T(8,128)}) custom-call(s32[4]{0:T(128)} %and_select_fusion.1.refs_0_, f32[4,576,384]{2,1,0:T(8,128)} %get-tuple-element.102.refs_1_, bf16[4,576,1152]{2,1,0:T(8,128)(2,1)} %get-tuple-element.103.refs_2_, ...), custom_call_target="tpu_custom_call" | custom-call | flops 32000000000 | bytes 1048576 | tf_op jit(solution)/shard_map/sparse_backward/pallas_call | solution.py:322
  305.6 46.1 %exchange_back.3 = (bf16[4,128,384]{2,1,0:T(8,128)(2,1)}, bf16[8,128,768]{2,1,0:T(8,128)(2,1)}, bf16[8,128,768]{2,1,0:T(8,128)(2,1)}, bf16[8,128,384]{2,1,0:T(8,128)(2,1)}, f32[8,128]{1,0:T(8,128)}) custom-call(bf16[4,128,384]{2,1,0:T(8,128)(2,1)} %get-tuple-element.114.refs_0_, bf16[8,128,384]{2,1,0:T(8,128)(2,1)} %get-tuple-element.115.refs_1_.refs_0_, ...), custom_call_target="tpu_custom_call" | custom-call | flops 40000000000 | bytes 1048576 | tf_op jit(solution)/shard_map/exchange_back/pallas_call | solution.py:1170
  351.7 30.2 %sparse_backward.3 = (f32[4,576,384]{2,1,0:T(8,128)}, bf16[32,64,384]{2,1,0:T(8,128)(2,1)}, f32[8,384]{1,0:T(8,128)}) custom-call(s32[4]{0:T(128)} %and_select_fusion.1.refs_0_, f32[4,576,384]{2,1,0:T(8,128)} %get-tuple-element.92.refs_1_, bf16[4,576,1152]{2,1,0:T(8,128)(2,1)} %get-tuple-element.93.refs_2_, bf16[4,576,384]{2,1,0:T(8,128)(2,1)} %get-tuple-element.94.refs_3_, ...), custom_call_target="tpu_custom_call" | custom-call | flops 32000000000 | bytes 1048576 | tf_op jit(solution)/shard_map/sparse_backward/pallas_call | solution.py:322
  381.9 50.5 %first_backward.1 = (bf16[32,176,384]{2,1,0:T(8,128)(2,1)}, f32[8,384]{1,0:T(8,128)}, f32[208,384]{1,0:T(8,128)}, f32[576,384]{1,0:T(8,128)}) custom-call(s32[4]{0:T(128)} %and_select_fusion.1.refs_0_, bf16[4,576,768]{2,1,0:T(8,128)(2,1)} %select_dynamic-update-slice_fusion.refs_1_, f32[4,576,384]{2,1,0:T(8,128)} %get-tuple-element.88.refs_2_, ...), custom_call_target="tpu_custom_call" | custom-call | flops 32000000000 | bytes 1048576 | tf_op jit(solution)/shard_map/first_backward/pallas_call | solution.py:322
  436.1 2.4 add_convert_fusion
  444.8 100.6 %reduce_all.1 = (f32[352,384]{1,0:T(8,128)}, bf16[2,2,2,2,2,48,384]{6,5,4,3,2,1,0:T(8,128)(2,1)}, f32[8,128]{1,0:T(8,128)}) custom-call(bf16[2,2,2,2,2,176,384]{6,5,4,3,2,1,0:T(8,128)(2,1)} %bitcast.92, bf16[2,2,2,2,2,64,384]{6,5,4,3,2,1,0:T(8,128)(2,1)} %bitcast.96, bf16[2,2,2,2,2,64,384]{6,5,4,3,2,1,0:T(8,128)(2,1)} %bitcast.95, ...), custom_call_target="tpu_custom_call" | custom-call | flops 60000002048 | bytes 1048576 | tf_op jit(solution)/shard_map/reduce_all/pallas_call | solution.py:909
  556.4 2.2 multiply_subtract_fusion.3
  558.7 2.3 multiply_subtract_fusion.1
  562.4 3.1 multiply_subtract_fusion
  566.6 40.7 %expert_adam.2 = (f32[2,8,384,768]{3,2,1,0:T(8,128)}, f32[2,8,384,768]{3,2,1,0:T(8,128)}, f32[2,8,384,768]{3,2,1,0:T(8,128)}) custom-call(f32[1]{0:T(128)} %bitcast.35.scale_ref, f32[2,8,384,768]{3,2,1,0:T(8,128)} %w_ref.2, f32[2,8,384,768]{3,2,1,0:T(8,128)} %m_ref.2, f32[2,8,384,768]{3,2,1,0:T(8,128)} %s_ref.2, ...), custom_call_target="tpu_custom_call" | custom-call | tf_op jit(solution)/shard_map/expert_adam/pallas_call | solution.py:1233
  607.2 40.9 %expert_adam.3 = (f32[2,8,768,384]{3,2,1,0:T(8,128)}, f32[2,8,768,384]{3,2,1,0:T(8,128)}, f32[2,8,768,384]{3,2,1,0:T(8,128)}) custom-call(f32[1]{0:T(128)} %bitcast.35.scale_ref, f32[2,8,768,384]{3,2,1,0:T(8,128)} %w_ref.3, f32[2,8,768,384]{3,2,1,0:T(8,128)} %m_ref.3, f32[2,8,768,384]{3,2,1,0:T(8,128)} %s_ref.3, ...), custom_call_target="tpu_custom_call" | custom-call | tf_op jit(solution)/shard_map/expert_adam/pallas_call | solution.py:1233
  (139 shorter events, 45.5 us)
Async XLA Ops:
  7.2 4.2 copy-start.24
  7.2 6.7 %copy-start.13 = (f32[384,120]{0,1:T(8,128)S(1)}, f32[384,120]{0,1:T(8,128)}, u32[]{:S(2)}) copy-start(f32[384,120]{0,1:T(8,128)} %param.27) | copy-start | bytes 552964
  7.2 5.3 copy-start.11
  7.2 5.9 copy-start.19
  7.2 95.6 %all-gather.7.cloned.1.call-start = ((), (), s32[]{:S(2)}) async-start(), calls=%async_computation | async-start | bytes 1419264 | tf_op jit(solution)/shard_map/all_gather | solution.py:642
  12.0 41.0 %collective-permute-start = (s32[]{:T(128)}, s32[]{:T(128)}, u32[]{:S(2)}, u32[]{:S(2)}) collective-permute-start(s32[]{:T(128)} %reduce_sum.36), channel_id=1, source_target_pairs={{0,16},{16,0},{1,17},{17,1},{2,18},{18,2},{3,19},{19,3},{4,20},{20... | collective-permute-start | bytes 20 | tf_op jit(solution)/shard_map/ppermute | solution.py:1252
  13.9 150.6 %all-gather.9.cloned.1.call-start = ((), (), s32[]{:S(2)}) async-start(), calls=%async_computation.1 | async-start | bytes 1419264 | tf_op jit(solution)/shard_map/all_gather | solution.py:642
  14.6 38.1 %copy-start.5 = (f32[210,384]{1,0:T(8,128)S(1)}, f32[210,384]{1,0:T(8,128)}, u32[]{:S(2)}) copy-start(f32[210,384]{1,0:T(8,128)} %param.33) | copy-start | bytes 967684
  52.8 6.7 %slice-start.1 = ((f32[210,384]{1,0:T(8,128)}), f32[196,384]{1,0:T(8,128)S(1)}, s32[]{:S(2)}) async-start(f32[210,384]{1,0:T(8,128)} %param.33), calls=%async_computation.3 | async-start | bytes 614400 | tf_op jit(solution)/shard_map/slice | solution.py:1308
  56.9 3.6 copy-start.2
  59.2 16.7 %collective-permute-start.1 = (bf16[1,576,768]{2,1,0:T(8,128)(2,1)}, bf16[1,576,768]{2,1,0:T(8,128)(2,1)}, u32[]{:S(2)}, u32[]{:S(2)}) collective-permute-start(bf16[1,576,768]{2,1,0:T(8,128)(2,1)} %constant_dynamic-slice_fusion), channel_id=1, source_target_pairs={{0,16},{16,0},{1,17},{17,1},{2,18},{18,2},{3,19},{19,3},{4,20},{20... | collective-permute-start | bytes 2654216 | tf_op jit(solution)/shard_map/ppermute | solution.py:1258
  61.5 5.4 slice-start
  61.5 6.0 copy-start.6
  62.2 6.5 copy-start
  64.7 4.1 copy-start.4
  72.7 1.4 collective-permute-start.2
  381.9 54.2 %copy-start.1 = (f32[576,196]{0,1:T(8,128)S(1)}, f32[576,196]{0,1:T(8,128)}, u32[]{:S(2)}) copy-start(f32[576,196]{0,1:T(8,128)} %copy-done) | copy-start | bytes 1354756
  436.0 4.9 copy-start.21
  436.0 5.5 copy-start.22
  552.7 6.0 copy-start.7
  552.8 9.6 %copy-start.9 = (f32[385,1000]{1,0:T(8,128)S(1)}, f32[385,1000]{1,0:T(8,128)}, u32[]{:S(2)}) copy-start(f32[385,1000]{1,0:T(8,128)} %param.45) | copy-start | bytes 4620004
  554.6 6.3 copy-start.20
  556.4 5.9 copy-start.3
  556.4 5.9 copy-start.8
  (9 other events, 27.6 us)
Sparse Core Ops, SparseCore 0:
  14.0 58.9 all-gather.6
  76.4 53.5 all-gather.8
where the time goes:
time: 657 us; the launch traced here: 656 us
  Pallas kernels  565 us (86%)
  local copies, waits for them, and re-layouts  38 us (6%)
  other arithmetic  26.2 us (4%)
  between operations  22.6 us (3%)
    pallas_call x7, Pallas kernels, by_image(): pl.pallas_call(kernel, grid_spec=pltpu.PrefetchScalarGridSpec(num_scalar_...  181 us
    pallas_call x4, Pallas kernels, exchange(): pl.pallas_call(kernel, in_specs=in_specs, out_specs=[inside] * len(out_sh...  164 us
    pallas_call x1, Pallas kernels, reduce_all(): pl.pallas_call(kernel, in_specs=[pl.BlockSpec(memory_space=pl.ANY)] * cou...  101 us
    pallas_call x2, Pallas kernels, expert_adam(): pl.pallas_call(kernel, grid=(layers, local // each), in_specs=[pl.BlockSp...  81.5 us
    pallas_call x1, Pallas kernels, gather_all(): pl.pallas_call(kernel, in_specs=[pl.BlockSpec(memory_space=pltpu.VMEM)] *...  37.3 us
  transfers between devices with their start and end apart: 5, of which 1 were waited for; matrix products, arithmetic and copies ran while one was open for 4% of the time, Pallas kernels for 18%

commit v1 on v0

--- a/solution.py
+++ b/solution.py
@@ -1248,15 +1248,19 @@
     swap = [(0, 1), (1, 0)]
     images = resolution.shape[0]
     place = jnp.arange(images, dtype=jnp.int32)
-    count = jnp.sum(resolution)
-    other = lax.ppermute(count, "dp", swap)
+    facts = lax.ppermute(jnp.stack([resolution, labels]), "dp", swap)
+    count, other = jnp.sum(resolution), jnp.sum(facts[0])
     moves = jnp.abs(count - other) >= 2
     wanted = (count > other).astype(jnp.int32)
-    at = jnp.min(jnp.where(resolution == wanted, place, images - 1))
+
+    def first_of(numbers, value):
+        return jnp.min(jnp.where(numbers == value, place, images - 1))
+
+    at = first_of(resolution, wanted)
     chosen = place == at
     out = lax.dynamic_slice_in_dim(patches, at, 1, 0)
     got = lax.ppermute(out, "dp", swap)
-    label = lax.ppermute(jnp.sum(jnp.where(chosen, labels, 0)), "dp", swap)
+    label = jnp.sum(jnp.where(place == first_of(facts[0], 1 - wanted), facts[1], 0))
     patches = lax.dynamic_update_slice_in_dim(patches, jnp.where(moves, got, out), at, 0)
     moved = chosen & moves
     return (

time: 657 us -> 658 us (level); the launches traced: 656 us -> 650 us
  Pallas kernels: 565 us -> 556 us
    pallas_call x7, Pallas kernels: 181 us -> 222 us  [by_image(): pl.pallas_call(kernel, grid_spec=pltpu.PrefetchScalarGridSpec(num_scalar_...]
    pallas_call x4, Pallas kernels: 164 us -> 136 us  [exchange(): pl.pallas_call(kernel, in_specs=in_specs, out_specs=[inside] * len(out_sh...]
    pallas_call x1, Pallas kernels: 101 us -> 79.7 us  [reduce_all(): pl.pallas_call(kernel, in_specs=[pl.BlockSpec(memory_space=pl.ANY)] * cou...]
  transfers between devices with their start and end apart: 5 -> 4, of which waited for: 1 -> 0; matrix products, arithmetic and copies ran while one was open for 4% -> 5% of each run, Pallas kernels for 18% -> 18%
where the time goes in v1:
time: 658 us; the launch traced here: 650 us
  Pallas kernels  556 us (84%)
  local copies, waits for them, and re-layouts  38.5 us (6%)
  other arithmetic  27.5 us (4%)
  between operations  22.7 us (3%)
    pallas_call x7, Pallas kernels, by_image(): pl.pallas_call(kernel, grid_spec=pltpu.PrefetchScalarGridSpec(num_scalar_...  222 us
    pallas_call x4, Pallas kernels, exchange(): pl.pallas_call(kernel, in_specs=in_specs, out_specs=[inside] * len(out_sh...  136 us
    pallas_call x2, Pallas kernels, expert_adam(): pl.pallas_call(kernel, grid=(layers, local // each), in_specs=[pl.BlockSp...  81.6 us
    pallas_call x1, Pallas kernels, reduce_all(): pl.pallas_call(kernel, in_specs=[pl.BlockSpec(memory_space=pl.ANY)] * cou...  79.7 us
    pallas_call x1, Pallas kernels, gather_all(): pl.pallas_call(kernel, in_specs=[pl.BlockSpec(memory_space=pltpu.VMEM)] *...  37.3 us
  transfers between devices with their start and end apart: 4, of which 0 were waited for; matrix products, arithmetic and copies ran while one was open for 5% of the time, Pallas kernels for 18%

profile of v1, /device:TPU:0, one launch (start us, length us, event | category | flops | bytes accessed | tf_op | source)
XLA Modules:
  0.0 650.3 jit_solution(8524876130974891823)
XLA Ops:
  7.3 4.1 copy.89
  14.1 37.3 %gather_all.1 = (bf16[2,2,2,2,2,120,384]{6,5,4,3,2,1,0:T(8,128)(2,1)}, bf16[2,2,2,2,2,48,384]{6,5,4,3,2,1,0:T(8,128)(2,1)}) custom-call(bf16[120,384]{1,0:T(8,128)(2,1)} %convert_bitcast_fusion.2.refs_0_, bf16[48,384]{1,0:T(8,128)(2,1)} %get-tuple-element.241.refs_1_), custom_call_target="tpu_custom_call" | custom-call | flops 40000000000 | bytes 1048576 | tf_op jit(solution)/shard_map/gather_all/pallas_call | solution.py:787
  54.5 2.2 convolution_bitcast_fusion
  78.5 2.3 select_dynamic-update-slice_fusion.refs_1_
  80.7 29.7 %first_forward.1 = (f32[4,576,384]{2,1,0:T(8,128)}, bf16[4,576,1152]{2,1,0:T(8,128)(2,1)}, bf16[4,576,384]{2,1,0:T(8,128)(2,1)}, f32[4,576,384]{2,1,0:T(8,128)}, f32[4,576,384]{2,1,0:T(8,128)}) custom-call(s32[4]{0:T(128)} %subtract_select_fusion.refs_0_, bf16[4,576,768]{2,1,0:T(8,128)(2,1)} %select_dynamic-update-slice_fusion.refs_1_, ...), custom_call_target="tpu_custom_call" | custom-call | flops 32000000000 | bytes 1048576 | tf_op jit(solution)/shard_map/first_forward/pallas_call | solution.py:322
  112.4 2.4 slice.169
  114.8 20.0 %sparse_forward.2 = (bf16[4,576,1152]{2,1,0:T(8,128)(2,1)}, bf16[4,576,384]{2,1,0:T(8,128)(2,1)}, f32[4,576,384]{2,1,0:T(8,128)}, bf16[4,576,128]{2,1,0:T(8,128)(2,1)}, bf16[4,128,384]{2,1,0:T(8,128)(2,1)}) custom-call(s32[4]{0:T(128)} %subtract_select_fusion.refs_0_, f32[4,576,384]{2,1,0:T(8,128)} %get-tuple-element.92.refs_1_, bf16[1536,384]{1,0:T(8,128)(2,1)} %bitcast.90, ...), custom_call_target="tpu_custom_call" | custom-call | flops 32000000000 | bytes 1048576 | tf_op jit(solution)/shard_map/sparse_forward/pallas_call | solution.py:322
  134.8 31.2 %exchange.2 = (bf16[4,128,384]{2,1,0:T(8,128)(2,1)}, bf16[8,128,384]{2,1,0:T(8,128)(2,1)}) custom-call(bf16[4,128,384]{2,1,0:T(8,128)(2,1)} %get-tuple-element.98.refs_0_, f32[2,8,384,768]{3,2,1,0:T(8,128)} %w_ref.2, f32[2,8,768,384]{3,2,1,0:T(8,128)} %w_ref.3), custom_call_target="tpu_custom_call" | custom-call | flops 40000000000 | bytes 1048576 | tf_op jit(solution)/shard_map/exchange/pallas_call | solution.py:1170
  166.1 2.4 slice.137
  170.5 20.9 %sparse_forward.3 = (f32[4,576,384]{2,1,0:T(8,128)}, bf16[4,576,1152]{2,1,0:T(8,128)(2,1)}, bf16[4,576,384]{2,1,0:T(8,128)(2,1)}, f32[4,576,384]{2,1,0:T(8,128)}...) custom-call(s32[4]{0:T(128)} %subtract_select_fusion.refs_0_, ...), custom_call_target="tpu_custom_call" | custom-call | flops 32000000000 | bytes 1048576 | tf_op jit(solution)/shard_map/sparse_forward/pallas_call | solution.py:322
  191.3 33.0 %exchange.3 = (bf16[4,128,384]{2,1,0:T(8,128)(2,1)}, bf16[8,128,384]{2,1,0:T(8,128)(2,1)}) custom-call(bf16[4,128,384]{2,1,0:T(8,128)(2,1)} %get-tuple-element.107.refs_0_, f32[2,8,384,768]{3,2,1,0:T(8,128)} %w_ref.2, f32[2,8,768,384]{3,2,1,0:T(8,128)} %w_ref.3), custom_call_target="tpu_custom_call" | custom-call | flops 40000000000 | bytes 1048576 | tf_op jit(solution)/shard_map/exchange/pallas_call | solution.py:1170
  224.4 11.4 %top.1 = (f32[4,576,384]{2,1,0:T(8,128)}, bf16[4,128,384]{2,1,0:T(8,128)(2,1)}, bf16[32,32,384]{2,1,0:T(8,128)(2,1)}, f32[8,1024]{1,0:T(8,128)}, f32[8,384]{1,0:T(8,128)}, /*index=5*/f32[8,128]{1,0:T(8,128)}) custom-call(s32[4]{0:T(128)} %subtract_select_fusion.refs_0_, s32[4]{0:T(128)} %broadcast_select_fusion.refs_1_, ...), custom_call_target="tpu_custom_call" | custom-call | flops 32000000000 | bytes 1048576 | tf_op jit(solution)/shard_map/top/pallas_call | solution.py:322
  235.7 36.1 %exchange_back.2 = (bf16[4,128,384]{2,1,0:T(8,128)(2,1)}, bf16[8,128,768]{2,1,0:T(8,128)(2,1)}, bf16[8,128,768]{2,1,0:T(8,128)(2,1)}, bf16[8,128,384]{2,1,0:T(8,128)(2,1)}, f32[8,128]{1,0:T(8,128)}) custom-call(bf16[4,128,384]{2,1,0:T(8,128)(2,1)} %get-tuple-element.110.refs_0_, bf16[8,128,384]{2,1,0:T(8,128)(2,1)} %get-tuple-element.111.refs_1_, ...), custom_call_target="tpu_custom_call" | custom-call | flops 40000000000 | bytes 1048576 | tf_op jit(solution)/shard_map/exchange_back/pallas_call | solution.py:1170
  271.8 39.5 %sparse_backward.2 = (f32[4,576,384]{2,1,0:T(8,128)}, bf16[4,128,384]{2,1,0:T(8,128)(2,1)}, bf16[32,64,384]{2,1,0:T(8,128)(2,1)}, f32[8,384]{1,0:T(8,128)}) custom-call(s32[4]{0:T(128)} %subtract_select_fusion.refs_0_, f32[4,576,384]{2,1,0:T(8,128)} %get-tuple-element.102.refs_1_, bf16[4,576,1152]{2,1,0:T(8,128)(2,1)} %get-tuple-element.103.refs_2_, ...), custom_call_target="tpu_custom_call" | custom-call | flops 32000000000 | bytes 1048576 | tf_op jit(solution)/shard_map/sparse_backward/pallas_call | solution.py:322
  311.3 35.2 %exchange_back.3 = (bf16[4,128,384]{2,1,0:T(8,128)(2,1)}, bf16[8,128,768]{2,1,0:T(8,128)(2,1)}, bf16[8,128,768]{2,1,0:T(8,128)(2,1)}, bf16[8,128,384]{2,1,0:T(8,128)(2,1)}, f32[8,128]{1,0:T(8,128)}) custom-call(bf16[4,128,384]{2,1,0:T(8,128)(2,1)} %get-tuple-element.114.refs_0_, bf16[8,128,384]{2,1,0:T(8,128)(2,1)} %get-tuple-element.115.refs_1_.refs_0_, ...), custom_call_target="tpu_custom_call" | custom-call | flops 40000000000 | bytes 1048576 | tf_op jit(solution)/shard_map/exchange_back/pallas_call | solution.py:1170
  346.6 38.4 %sparse_backward.3 = (f32[4,576,384]{2,1,0:T(8,128)}, bf16[32,64,384]{2,1,0:T(8,128)(2,1)}, f32[8,384]{1,0:T(8,128)}) custom-call(s32[4]{0:T(128)} %subtract_select_fusion.refs_0_, f32[4,576,384]{2,1,0:T(8,128)} %get-tuple-element.92.refs_1_, bf16[4,576,1152]{2,1,0:T(8,128)(2,1)} %get-tuple-element.93.refs_2_, ...), custom_call_target="tpu_custom_call" | custom-call | flops 32000000000 | bytes 1048576 | tf_op jit(solution)/shard_map/sparse_backward/pallas_call | solution.py:322
  385.0 62.1 %first_backward.1 = (bf16[32,176,384]{2,1,0:T(8,128)(2,1)}, f32[8,384]{1,0:T(8,128)}, f32[208,384]{1,0:T(8,128)}, f32[576,384]{1,0:T(8,128)}) custom-call(s32[4]{0:T(128)} %subtract_select_fusion.refs_0_, bf16[4,576,768]{2,1,0:T(8,128)(2,1)} %select_dynamic-update-slice_fusion.refs_1_, f32[4,576,384]{2,1,0:T(8,128)} %get-tuple-element.88.refs_2_, ...), custom_call_target="tpu_custom_call" | custom-call | flops 32000000000 | bytes 1048576 | tf_op jit(solution)/shard_map/first_backward/pallas_call | solution.py:322
  450.8 2.4 add_convert_fusion
  459.5 79.7 %reduce_all.1 = (f32[352,384]{1,0:T(8,128)}, bf16[2,2,2,2,2,48,384]{6,5,4,3,2,1,0:T(8,128)(2,1)}, f32[8,128]{1,0:T(8,128)}) custom-call(bf16[2,2,2,2,2,176,384]{6,5,4,3,2,1,0:T(8,128)(2,1)} %bitcast.102, bf16[2,2,2,2,2,64,384]{6,5,4,3,2,1,0:T(8,128)(2,1)} %bitcast.106, bf16[2,2,2,2,2,64,384]{6,5,4,3,2,1,0:T(8,128)(2,1)} %bitcast.105, ...), custom_call_target="tpu_custom_call" | custom-call | flops 60000002048 | bytes 1048576 | tf_op jit(solution)/shard_map/reduce_all/pallas_call | solution.py:909
  550.2 2.2 multiply_subtract_fusion.3
  552.5 2.3 multiply_subtract_fusion.1
  556.3 3.1 multiply_subtract_fusion
  560.4 40.7 %expert_adam.2 = (f32[2,8,384,768]{3,2,1,0:T(8,128)}, f32[2,8,384,768]{3,2,1,0:T(8,128)}, f32[2,8,384,768]{3,2,1,0:T(8,128)}) custom-call(f32[1]{0:T(128)} %bitcast.39.scale_ref, f32[2,8,384,768]{3,2,1,0:T(8,128)} %w_ref.2, f32[2,8,384,768]{3,2,1,0:T(8,128)} %m_ref.2, f32[2,8,384,768]{3,2,1,0:T(8,128)} %s_ref.2, ...), custom_call_target="tpu_custom_call" | custom-call | tf_op jit(solution)/shard_map/expert_adam/pallas_call | solution.py:1233
  601.1 40.9 %expert_adam.3 = (f32[2,8,768,384]{3,2,1,0:T(8,128)}, f32[2,8,768,384]{3,2,1,0:T(8,128)}, f32[2,8,768,384]{3,2,1,0:T(8,128)}) custom-call(f32[1]{0:T(128)} %bitcast.39.scale_ref, f32[2,8,768,384]{3,2,1,0:T(8,128)} %w_ref.3, f32[2,8,768,384]{3,2,1,0:T(8,128)} %m_ref.3, f32[2,8,768,384]{3,2,1,0:T(8,128)} %s_ref.3, ...), custom_call_target="tpu_custom_call" | custom-call | tf_op jit(solution)/shard_map/expert_adam/pallas_call | solution.py:1233
  (137 shorter events, 48.2 us)
Async XLA Ops:
  7.2 4.2 copy-start.23
  7.2 4.2 copy-start.22
  7.2 6.2 copy-start.12
  7.2 4.7 copy-start.10
  7.2 5.4 copy-start.18
  7.2 103.2 %all-gather.7.cloned.1.call-start = ((), (), s32[]{:S(2)}) async-start(), calls=%async_computation | async-start | bytes 1419264 | tf_op jit(solution)/shard_map/all_gather | solution.py:642
  11.4 45.3 %collective-permute-start = (s32[2,4]{1,0:T(2,128)S(1)}, s32[2,4]{1,0:T(2,128)S(1)}, u32[]{:S(2)}, u32[]{:S(2)}) collective-permute-start(s32[2,4]{1,0:T(2,128)S(1)} %pad_add_fusion), channel_id=1, source_target_pairs={{0,16},{16,0},{1,17},{17,1},{2,18},{18,2},{3,19},{19,3},{4,20},{20... | collective-permute-start | bytes 104 | tf_op jit(solution)/shard_map/ppermute | solution.py:1251
  13.3 152.7 %all-gather.9.cloned.1.call-start = ((), (), s32[]{:S(2)}) async-start(), calls=%async_computation.1 | async-start | bytes 1419264 | tf_op jit(solution)/shard_map/all_gather | solution.py:642
  14.1 38.0 %copy-start.5 = (f32[210,384]{1,0:T(8,128)S(1)}, f32[210,384]{1,0:T(8,128)}, u32[]{:S(2)}) copy-start(f32[210,384]{1,0:T(8,128)} %param.33) | copy-start | bytes 967684
  54.5 8.9 %copy-start = (f32[576,196]{0,1:T(8,128)}, f32[576,196]{0,1:T(8,128)S(1)}, u32[]{:S(2)}) copy-start(f32[576,196]{0,1:T(8,128)S(1)} %mul.236) | copy-start | bytes 1354756
  56.7 8.1 %copy-start.2 = (f32[385,1000]{1,0:T(8,128)S(1)}, f32[385,1000]{1,0:T(8,128)}, u32[]{:S(2)}) copy-start(f32[385,1000]{1,0:T(8,128)} %param.32) | copy-start | bytes 4620004
  63.4 4.2 slice-start.1
  63.4 15.0 %collective-permute-start.1 = (bf16[1,576,768]{2,1,0:T(8,128)(2,1)}, bf16[1,576,768]{2,1,0:T(8,128)(2,1)}, u32[]{:S(2)}, u32[]{:S(2)}) collective-permute-start(bf16[1,576,768]{2,1,0:T(8,128)(2,1)} %constant_dynamic-slice_fusion), channel_id=1, source_target_pairs={{0,16},{16,0},{1,17},{17,1},{2,18},{18,2},{3,19},{19,3},{4,20},{20... | collective-permute-start | bytes 2654216 | tf_op jit(solution)/shard_map/ppermute | solution.py:1262
  64.8 5.5 slice-start
  64.8 6.1 copy-start.4
  385.0 65.7 %copy-start.1 = (f32[576,196]{0,1:T(8,128)S(1)}, f32[576,196]{0,1:T(8,128)}, u32[]{:S(2)}) copy-start(f32[576,196]{0,1:T(8,128)} %copy-done) | copy-start | bytes 1354756
  450.8 4.9 copy-start.20
  450.8 5.5 copy-start.21
  542.6 3.3 copy-start.9
  546.5 6.0 copy-start.6
  546.6 9.6 %copy-start.8 = (f32[385,1000]{1,0:T(8,128)S(1)}, f32[385,1000]{1,0:T(8,128)}, u32[]{:S(2)}) copy-start(f32[385,1000]{1,0:T(8,128)} %param.45) | copy-start | bytes 4620004
  548.5 6.3 copy-start.19
  550.2 5.9 copy-start.3
  550.2 5.9 copy-start.7
  (6 other events, 19.1 us)
Sparse Core Ops, SparseCore 0:
  13.5 58.9 all-gather.6
  75.9 53.5 all-gather.8
